TPU v7x, 128 devices: a whole 4x4x4 slice. The times are simulated.
128 devices in a mesh: row: 16 (over x, z), partner: 4 (over y), feat: 2 (over core).
Axes of the slice: x: 4, y: 4, z: 4, core: 2. Of those that a mesh axis runs over, the one named last changes fastest.
Arguments:
- embeddings: bfloat16 [1048576, 256], P(('row', 'partner'), 'feat'), may hold values from -1.5 to 1.5
- decoder_gain: float32 [256], P('feat'), may hold values from 0.5 to 2
- block_pairs: int32 [64, 64, 2, 2], replicated, may hold values from 0 to 8191, as said below
- pair_counts: int32 [64, 64], replicated, may hold values from 0 to 2, as said below
- edge_labels: bfloat16 [64, 64, 2, 128, 128], P(('row', 'partner')), may hold values from 0 to 1, as said below
Outputs:
- grad_embeddings: float32 [1048576, 256], P(('row', 'partner'), 'feat')
- grad_gain: float32 [256], P('feat')
Inputs may be any that keep to these rules, and one draw needn't show every extreme that they name: pair_counts[r, o] is 0 for o < r, 2 for o = r and 1 to 2 for o > r. block_pairs[r, o, c, 0] is a block of requester r (r * 128 to (r + 1) * 128 - 1) and block_pairs[r, o, c, 1] a block of owner o; in live slots the row block is at most the column block. `edge_labels`: every entry is 0 or 1.
All inputs are finite; a program needn't handle non-finite values.
Results may differ from a plain program's by a relative error of at most 0.0044.
Values may be sent and summed in bfloat16 or wider, within the bound.
A program may use at most 128 MiB of HBM per device.

v0:
```python
import jax
import jax.numpy as jnp
from jax import lax
from jax.sharding import PartitionSpec as P

OWNER_STEP = 8


def tile_logits(rows_scaled, cols_in):
    partial_logits = jnp.einsum(
        "sik,sjk->sij", rows_scaled, cols_in, preferred_element_type=jnp.float32
    )
    return lax.psum(partial_logits, "feat")


def tile_grads(rows_scaled, cols_in, target_tiles, live_mask, decoder_gain):
    logits = tile_logits(rows_scaled, cols_in)
    residual = (jax.nn.sigmoid(logits) - target_tiles.astype(jnp.float32)) * live_mask[
        :, None, None
    ].astype(jnp.float32)
    residual = residual.astype(jnp.bfloat16)
    pulled = jnp.einsum("sij,sjk->sik", residual, cols_in, preferred_element_type=jnp.float32)
    row_terms = (pulled * decoder_gain[None, None, :]).astype(jnp.bfloat16)
    col_terms = jnp.einsum(
        "sij,sik->sjk", residual, rows_scaled, preferred_element_type=jnp.float32
    ).astype(jnp.bfloat16)
    return (pulled, row_terms, col_terms)


def widen(values):
    return lax.optimization_barrier(values).astype(jnp.float32)


def local(embeddings, decoder_gain, block_pairs, pair_counts, edge_labels):
    grid_rows = lax.axis_size("row")
    grid_cols = lax.axis_size("partner")
    owner_count = grid_rows * grid_cols
    self_index = lax.axis_index(("row", "partner"))
    tile_rows = edge_labels.shape[-1]
    half_width = embeddings.shape[1]
    blocks_dev = embeddings.shape[0] // tile_rows
    slot_count = block_pairs.shape[2]
    resident = embeddings.reshape(blocks_dev, tile_rows, half_width)
    scaled = (embeddings.astype(jnp.float32) * decoder_gain[None, :]).astype(jnp.bfloat16)
    scaled = scaled.reshape(blocks_dev, tile_rows, half_width)
    my_labels = edge_labels.reshape(owner_count, slot_count, tile_rows, tile_rows)
    positions = jnp.arange(slot_count)
    base_block = self_index * blocks_dev
    pairs_as_req = lax.dynamic_index_in_dim(block_pairs, self_index, 0, keepdims=False)
    pairs_as_own = lax.dynamic_index_in_dim(block_pairs, self_index, 1, keepdims=False)
    group_tiles = OWNER_STEP * slot_count
    zero_acc = jnp.zeros((blocks_dev, tile_rows, half_width), jnp.float32)
    zero_back = jnp.zeros((owner_count, slot_count, tile_rows, half_width), jnp.bfloat16)
    zero_gain = jnp.zeros((half_width,), jnp.float32)
    col_ids = (pairs_as_own[:, :, 1] - base_block).reshape(-1)
    outgoing = jnp.take(resident, col_ids, axis=0).reshape(
        owner_count, slot_count, tile_rows, half_width
    )
    fetched = lax.all_to_all(outgoing, ("row", "partner"), split_axis=0, concat_axis=0, tiled=True)
    row_ids = pairs_as_req[:, :, 0] - base_block
    live_counts = lax.dynamic_index_in_dim(pair_counts, self_index, 0, keepdims=False)

    def group_step(group_index, state_triple):
        row_acc, returned, gain_part = state_triple
        first_owner = group_index * OWNER_STEP
        cols_in = lax.dynamic_slice_in_dim(fetched, first_owner, OWNER_STEP, 0).reshape(
            group_tiles, tile_rows, half_width
        )
        rows_here = lax.dynamic_slice_in_dim(row_ids, first_owner, OWNER_STEP, 0).reshape(
            group_tiles
        )
        have_count = lax.dynamic_slice_in_dim(live_counts, first_owner, OWNER_STEP, 0)
        live_mask = (positions[None, :] < have_count[:, None]).reshape(group_tiles)
        target_tiles = lax.dynamic_slice_in_dim(my_labels, first_owner, OWNER_STEP, 0).reshape(
            group_tiles, tile_rows, tile_rows
        )
        rows_in = jnp.take(resident, rows_here, axis=0)
        rows_scaled = jnp.take(scaled, rows_here, axis=0)
        pulled, row_terms, col_terms = tile_grads(
            rows_scaled, cols_in, target_tiles, live_mask, decoder_gain
        )
        row_acc = row_acc.at[rows_here].add(widen(row_terms))
        gain_part = gain_part + jnp.sum(rows_in.astype(jnp.float32) * pulled, axis=(0, 1))
        returned = lax.dynamic_update_slice_in_dim(
            returned,
            col_terms.reshape(OWNER_STEP, slot_count, tile_rows, half_width),
            first_owner,
            0,
        )
        return (row_acc, returned, gain_part)

    row_acc, returned, gain_part = lax.fori_loop(
        0, owner_count // OWNER_STEP, group_step, (zero_acc, zero_back, zero_gain)
    )
    returned_back = lax.all_to_all(
        returned, ("row", "partner"), split_axis=0, concat_axis=0, tiled=True
    )
    grad_sum = row_acc.at[col_ids].add(
        returned_back.reshape(owner_count * slot_count, tile_rows, half_width).astype(jnp.float32)
    )
    gain_total = lax.psum(gain_part, ("row", "partner"))
    grad_gain = gain_total * (16.0 / (owner_count * tile_rows))
    return (grad_sum.reshape(blocks_dev * tile_rows, half_width), grad_gain)


def solution(mesh):
    in_specs = (
        P(("row", "partner"), "feat"),
        P("feat"),
        P(),
        P(),
        P(("row", "partner"), None, None, None, None),
    )
    out_specs = (P(("row", "partner"), "feat"), P("feat"))
    return jax.shard_map(local, mesh=mesh, in_specs=in_specs, out_specs=out_specs, check_vma=False)
```

profile of v0, /device:TPU:8, one launch (start us, length us, event | category | flops | bytes accessed | tf_op | source)
XLA Modules:
  0.0 676.4 jit_solution(10251011161050612187)
XLA Ops:
  8.8 5.3 gather_fusion.2
  14.1 4.6 broadcast_select_fusion.4
  18.7 11.7 %all-to-all-start = ((bf16[64,2,128,128]{3,2,1,0:T(8,128)(2,1)}), bf16[64,2,128,128]{3,2,1,0:T(8,128)(2,1)}, u32[]{:S(2)}, u32[]{:S(2)}) async-start(bf16[64,2,128,128]{3,2,1,0:T(8,128)(2,1)} %broadcast_select_fusion.4), calls=%async_computation | async-start | bytes 8388608 | tf_op jit(solution)/shard_map/all_to_all | solution.py:59
  31.2 4.0 multiply_convert_fusion.1
  35.2 50.3 %all-to-all-done = bf16[64,2,128,128]{3,2,1,0:T(8,128)(2,1)} async-done(((bf16[64,2,128,128]{3,2,1,0:T(8,128)(2,1)}), bf16[64,2,128,128]{3,2,1,0:T(8,128)(2,1)}, u32[]{:S(2)}, u32[]{:S(2)}) %all-to-all-start) | async-done | bytes 4194336 | tf_op jit(solution)/shard_map/all_to_all | solution.py:59
  85.5 3.0 broadcast_in_dim.43
  88.5 4.5 broadcast_in_dim.42
  92.9 315.9 %while.18 = (s32[]{:T(128)}, f32[128,128,128]{2,1,0:T(8,128)}, bf16[64,2,128,128]{3,2,1,0:T(8,128)(2,1)}, f32[128]{0:T(128)S(1)}, s32[64,2]{0,1:T(2,128)S(1)}, /...) while((s32[]{:T(128)}, f32[128,128,128]{2,1,0:T(8,128)}, ...), condition=%wide.region_4.6_spmd.clone, body=%wide.region_0.5_spmd.clone.sunk | while | flops 206308704 | bytes 24125664 | solution.py:92
  93.2 1.1 constant_dynamic-slice_fusion.9
  94.3 2.8 gather_fusion.1
  97.1 1.5 fusion.30
  99.0 2.8 gather_fusion
  102.9 25.5 %all-reduce.2.cloned.1.call-done = f32[16,128,128]{2,1,0:T(8,128)} async-done(((f32[16,128,128]{2,1,0:T(8,128)}), f32[16,128,128]{2,1,0:T(8,128)}) %all-reduce.2.cloned.1.call-update) | async-done | bytes 1048592 | tf_op jit(solution)/shard_map/while/body/eval_jaxpr/psum | solution.py:13
  128.5 1.5 fusion.32
  131.8 3.4 scatter_fusion
  135.4 1.1 constant_dynamic-slice_fusion.9
  136.5 2.8 gather_fusion.1
  139.4 1.5 fusion.30
  141.2 2.8 gather_fusion
  145.2 22.4 %all-reduce.2.cloned.1.call-done = f32[16,128,128]{2,1,0:T(8,128)} async-done(((f32[16,128,128]{2,1,0:T(8,128)}), f32[16,128,128]{2,1,0:T(8,128)}) %all-reduce.2.cloned.1.call-update) | async-done | bytes 1048592 | tf_op jit(solution)/shard_map/while/body/eval_jaxpr/psum | solution.py:13
  167.6 1.5 fusion.32
  170.9 3.3 scatter_fusion
  174.5 1.1 constant_dynamic-slice_fusion.9
  175.6 2.8 gather_fusion.1
  178.5 1.5 fusion.30
  180.3 2.8 gather_fusion
  184.3 22.4 %all-reduce.2.cloned.1.call-done = f32[16,128,128]{2,1,0:T(8,128)} async-done(((f32[16,128,128]{2,1,0:T(8,128)}), f32[16,128,128]{2,1,0:T(8,128)}) %all-reduce.2.cloned.1.call-update) | async-done | bytes 1048592 | tf_op jit(solution)/shard_map/while/body/eval_jaxpr/psum | solution.py:13
  206.7 1.5 fusion.32
  210.0 3.3 scatter_fusion
  213.6 1.1 constant_dynamic-slice_fusion.9
  214.7 2.8 gather_fusion.1
  217.5 1.5 fusion.30
  219.4 2.8 gather_fusion
  223.3 22.4 %all-reduce.2.cloned.1.call-done = f32[16,128,128]{2,1,0:T(8,128)} async-done(((f32[16,128,128]{2,1,0:T(8,128)}), f32[16,128,128]{2,1,0:T(8,128)}) %all-reduce.2.cloned.1.call-update) | async-done | bytes 1048592 | tf_op jit(solution)/shard_map/while/body/eval_jaxpr/psum | solution.py:13
  245.7 1.5 fusion.32
  249.0 3.4 scatter_fusion
  253.8 2.8 gather_fusion.1
  256.6 1.5 fusion.30
  258.4 2.8 gather_fusion
  262.4 22.4 %all-reduce.2.cloned.1.call-done = f32[16,128,128]{2,1,0:T(8,128)} async-done(((f32[16,128,128]{2,1,0:T(8,128)}), f32[16,128,128]{2,1,0:T(8,128)}) %all-reduce.2.cloned.1.call-update) | async-done | bytes 1048592 | tf_op jit(solution)/shard_map/while/body/eval_jaxpr/psum | solution.py:13
  284.8 1.5 fusion.32
  288.1 3.4 scatter_fusion
  292.9 2.8 gather_fusion.1
  295.7 1.5 fusion.30
  297.6 2.8 gather_fusion
  301.5 22.4 %all-reduce.2.cloned.1.call-done = f32[16,128,128]{2,1,0:T(8,128)} async-done(((f32[16,128,128]{2,1,0:T(8,128)}), f32[16,128,128]{2,1,0:T(8,128)}) %all-reduce.2.cloned.1.call-update) | async-done | bytes 1048592 | tf_op jit(solution)/shard_map/while/body/eval_jaxpr/psum | solution.py:13
  323.9 1.5 fusion.32
  327.3 3.3 scatter_fusion
  332.0 2.8 gather_fusion.1
  334.8 1.5 fusion.30
  336.7 2.8 gather_fusion
  340.6 22.4 %all-reduce.2.cloned.1.call-done = f32[16,128,128]{2,1,0:T(8,128)} async-done(((f32[16,128,128]{2,1,0:T(8,128)}), f32[16,128,128]{2,1,0:T(8,128)}) %all-reduce.2.cloned.1.call-update) | async-done | bytes 1048592 | tf_op jit(solution)/shard_map/while/body/eval_jaxpr/psum | solution.py:13
  363.0 1.5 fusion.32
  366.3 3.4 scatter_fusion
  371.1 2.8 gather_fusion.1
  373.9 1.5 fusion.30
  375.8 2.8 gather_fusion
  379.7 22.4 %all-reduce.2.cloned.1.call-done = f32[16,128,128]{2,1,0:T(8,128)} async-done(((f32[16,128,128]{2,1,0:T(8,128)}), f32[16,128,128]{2,1,0:T(8,128)}) %all-reduce.2.cloned.1.call-update) | async-done | bytes 1048592 | tf_op jit(solution)/shard_map/while/body/eval_jaxpr/psum | solution.py:13
  402.1 1.5 fusion.32
  405.4 3.4 scatter_fusion
  408.8 10.6 %all-to-all-start.1 = ((bf16[64,2,128,128]{3,2,1,0:T(8,128)(2,1)}), bf16[64,2,128,128]{3,2,1,0:T(8,128)(2,1)}, u32[]{:S(2)}, u32[]{:S(2)}) async-start(bf16[64,2,128,128]{3,2,1,0:T(8,128)(2,1)} %get-tuple-element.205), calls=%async_computation.1 | async-start | bytes 8388608 | tf_op jit(solution)/shard_map/all_to_all | solution.py:95
  419.4 217.0 %psum.18 = f32[128]{0:T(128)S(1)} all-reduce(f32[128]{0:T(128)S(1)} %get-tuple-element.206), channel_id=1, replica_groups=mesh['row'=16,'partner'=4,'feat'=2] {'row','partner'}, use_global_device_ids=true, to_apply=%region_6.8 | all-reduce | flops 128 | bytes 1024 | tf_op jit(solution)/shard_map/psum | solution.py:101
  636.8 6.5 bitcast_convert_fusion
  643.3 26.2 %scatter_fusion.1 = f32[128,128,128]{2,1,0:T(8,128)} fusion(f32[128,128,128]{2,1,0:T(8,128)} %get-tuple-element.204, s32[128]{0:T(128)S(1)} %fusion.11, f32[128,128,128]{2,1,0:T(8,128)} %bitcast_convert_fusion), kind=kCustom, calls=%fused_computation.4 | custom fusion | flops 2097152 | bytes 25166336 | tf_op jit(solution)/shard_map/scatter-add | solution.py:98
  (175 shorter events, 34.8 us)
Async XLA Ops:
  7.2 0.9 copy-start
  18.7 12.5 %copy-start.1 = (f32[128]{0:T(128)S(1)}, f32[128]{0:T(128)}, u32[]{:S(2)}) copy-start(f32[128]{0:T(128)} %param.10) | copy-start | bytes 1540
  18.7 66.7 %all-to-all-start = ((bf16[64,2,128,128]{3,2,1,0:T(8,128)(2,1)}), bf16[64,2,128,128]{3,2,1,0:T(8,128)(2,1)}, u32[]{:S(2)}, u32[]{:S(2)}) async-start(bf16[64,2,128,128]{3,2,1,0:T(8,128)(2,1)} %broadcast_select_fusion.4), calls=%async_computation | async-start | bytes 8388608 | tf_op jit(solution)/shard_map/all_to_all | solution.py:59
  92.9 35.5 %all-reduce.2.cloned.1.call-start = ((), (), s32[]{:S(2)}) async-start(), calls=%async_computation.2 | async-start | bytes 2097152 | tf_op jit(solution)/shard_map/while/body/eval_jaxpr/psum | solution.py:13
  135.2 32.4 %all-reduce.2.cloned.1.call-start = ((), (), s32[]{:S(2)}) async-start(), calls=%async_computation.2 | async-start | bytes 2097152 | tf_op jit(solution)/shard_map/while/body/eval_jaxpr/psum | solution.py:13
  174.3 32.4 %all-reduce.2.cloned.1.call-start = ((), (), s32[]{:S(2)}) async-start(), calls=%async_computation.2 | async-start | bytes 2097152 | tf_op jit(solution)/shard_map/while/body/eval_jaxpr/psum | solution.py:13
  213.3 32.4 %all-reduce.2.cloned.1.call-start = ((), (), s32[]{:S(2)}) async-start(), calls=%async_computation.2 | async-start | bytes 2097152 | tf_op jit(solution)/shard_map/while/body/eval_jaxpr/psum | solution.py:13
  252.4 32.4 %all-reduce.2.cloned.1.call-start = ((), (), s32[]{:S(2)}) async-start(), calls=%async_computation.2 | async-start | bytes 2097152 | tf_op jit(solution)/shard_map/while/body/eval_jaxpr/psum | solution.py:13
  291.5 32.4 %all-reduce.2.cloned.1.call-start = ((), (), s32[]{:S(2)}) async-start(), calls=%async_computation.2 | async-start | bytes 2097152 | tf_op jit(solution)/shard_map/while/body/eval_jaxpr/psum | solution.py:13
  330.6 32.4 %all-reduce.2.cloned.1.call-start = ((), (), s32[]{:S(2)}) async-start(), calls=%async_computation.2 | async-start | bytes 2097152 | tf_op jit(solution)/shard_map/while/body/eval_jaxpr/psum | solution.py:13
  369.7 32.4 %all-reduce.2.cloned.1.call-start = ((), (), s32[]{:S(2)}) async-start(), calls=%async_computation.2 | async-start | bytes 2097152 | tf_op jit(solution)/shard_map/while/body/eval_jaxpr/psum | solution.py:13
  408.8 228.1 %all-to-all-start.1 = ((bf16[64,2,128,128]{3,2,1,0:T(8,128)(2,1)}), bf16[64,2,128,128]{3,2,1,0:T(8,128)(2,1)}, u32[]{:S(2)}, u32[]{:S(2)}) async-start(bf16[64,2,128,128]{3,2,1,0:T(8,128)(2,1)} %get-tuple-element.205), calls=%async_computation.1 | async-start | bytes 8388608 | tf_op jit(solution)/shard_map/all_to_all | solution.py:95
Sparse Core Ops, SparseCore 0:
  98.8 29.6 all-reduce.1
  141.0 26.4 all-reduce.1
  180.1 26.5 all-reduce.1
  219.2 26.4 all-reduce.1
  258.3 26.5 all-reduce.1
  297.4 26.5 all-reduce.1
  336.5 26.5 all-reduce.1
  375.6 26.4 all-reduce.1
where the time goes:
time: 679 us; the launch traced here: 676 us
  waiting for transfers between devices  233 us (34%)
  blocking collectives  217 us (32%)
  local copies, waits for them, and re-layouts  88.3 us (13%)
  other arithmetic  82.7 us (12%)
  starting transfers between devices  22.3 us (3%)
  matrix products  18.6 us (3%)
  between operations  14.1 us (2%)
    psum x1, blocking collectives, local(): gain_total = lax.psum(gain_part, ('row', 'partner'))  217 us
    psum x8, waiting for transfers between devices, tile_logits(): return lax.psum(partial_logits, 'feat')  182 us
    all_to_all x1, waiting for transfers between devices, local(): lax.all_to_all(outgoing, ('row', 'partner'), split_axis=0, concat_axis=0,...  50.3 us
    scatter-add x8, other arithmetic, group_step(): row_acc = row_acc.at[rows_here].add(widen(row_terms))  26.9 us
    scatter-add x1, other arithmetic, local(): row_acc.at[col_ids]  26.2 us
    gather x8, local copies, waits for them, and re-layouts, group_step(): rows_in = jnp.take(resident, rows_here, axis=0)  22.7 us
    gather x8, local copies, waits for them, and re-layouts, group_step(): rows_scaled = jnp.take(scaled, rows_here, axis=0)  22.7 us
  transfers between devices with their start and end apart: 10, of which 9 were waited for; matrix products, arithmetic and copies ran while one was open for 6% of the time, Pallas kernels for 0%

commit v1 on v0

v1 whole, which is shorter than its diff:
```python
import functools

import jax
import jax.numpy as jnp
from jax import lax
from jax.experimental import pallas as pl
from jax.experimental.pallas import tpu as pltpu
from jax.sharding import PartitionSpec as P

GROUP = 4
NODE_SPLIT = 2
MESH = pl.DeviceIdType.MESH


def exchange_kernel(
    owners,
    partners,
    row_ids,
    col_ids,
    counts,
    gain_ref,
    emb_ref,
    labels_hbm,
    terms_hbm,
    gain_out,
    staged,
    cols,
    rows_send,
    rows_sib,
    labels,
    col_tiles,
    row_tiles,
    gains,
    gain_send,
    gain_sib,
    gain_all,
    col_send_sem,
    col_recv_sem,
    rows_send_sem,
    rows_recv_sem,
    label_sem,
    back_send_sem,
    row_send_sem,
    term_recv_sem,
    local_sem,
    small_send_sem,
    small_recv_sem,
    gain_send_sem,
    gain_recv_sem,
):
    groups = owners // GROUP
    me = lax.axis_index("row") * partners + lax.axis_index("partner")
    feat = lax.axis_index("feat")
    other = 1 - feat
    first_group = me // GROUP
    width = emb_ref.shape[-1]

    def device(chip, core):
        return (chip // partners, chip % partners, core)

    sibling = device(me, other)

    def remote(src, dst, send, recv, where):
        return pltpu.make_async_remote_copy(
            src_ref=src, dst_ref=dst, send_sem=send, recv_sem=recv,
            device_id=where, device_id_type=MESH,
        )

    def col_copy(chip, slot):
        return remote(
            staged.at[slot, chip], cols.at[me, feat], col_send_sem.at[slot, chip],
            col_recv_sem.at[me, feat], device(chip, slot),
        )

    def col_arrival(owner, half):
        return remote(
            staged.at[0, 0], cols.at[owner, half], col_send_sem.at[0, 0],
            col_recv_sem.at[owner, half], sibling,
        )

    def rows_copy(group):
        span = pl.ds(group * GROUP, GROUP)
        return remote(
            rows_send.at[span], rows_sib.at[span], rows_send_sem.at[group],
            rows_recv_sem.at[group], sibling,
        )

    def label_copy(group):
        span = pl.ds(group * GROUP, GROUP)
        return pltpu.make_async_copy(
            labels_hbm.at[span, feat], labels.at[span], label_sem.at[group]
        )

    def back_copy(owner, side):
        core = feat if side == 0 else other
        return remote(
            col_tiles.at[owner, side], terms_hbm.at[feat, me], back_send_sem.at[owner, side],
            term_recv_sem.at[feat, me], device(owner, core),
        )

    def back_own():
        return pltpu.make_async_copy(
            col_tiles.at[me, 0], terms_hbm.at[feat, me], local_sem.at[owners]
        )

    def row_own(owner):
        return pltpu.make_async_copy(
            row_tiles.at[owner, 0], terms_hbm.at[feat, owner + 1], local_sem.at[owner]
        )

    def row_copy(owner):
        return remote(
            row_tiles.at[owner, 1], terms_hbm.at[feat, owner + 1], row_send_sem.at[owner],
            term_recv_sem.at[feat, owner + 1], sibling,
        )

    def term_arrival(slot, place):
        return remote(
            col_tiles.at[0, 0], terms_hbm.at[slot, place], row_send_sem.at[0],
            term_recv_sem.at[slot, place], sibling,
        )

    gain_scale = remote(
        gain_ref, gains.at[feat], small_send_sem.at[0], small_recv_sem.at[0], sibling
    )
    gain_scale.start()
    gains[feat] = gain_ref[...]

    def send_cols(step, _):
        chip = me - step
        for slot in range(2):
            staged[slot, chip] = emb_ref[col_ids[slot, chip]]
            col_copy(chip, slot).start()
        return 0

    staged[other, me] = emb_ref[col_ids[other, me]]
    col_copy(me, other).start()
    cols[me, feat] = emb_ref[col_ids[feat, me]]
    lax.fori_loop(1, me + 1, send_cols, 0)

    def send_rows(group, _):
        label_copy(group).start()
        for j in range(GROUP):
            owner = group * GROUP + j
            rows_send[owner] = emb_ref[row_ids[other, owner]]
        rows_copy(group).start()
        return 0

    lax.fori_loop(first_group, groups, send_rows, 0)

    gain_scale.wait_recv()
    gain_pair = jnp.concatenate([gains[feat], gains[other]], axis=-1)[:1]

    def work(group, gain_sum):
        rows_copy(group).wait_recv()
        label_copy(group).wait()
        for j in range(GROUP):
            owner = group * GROUP + j

            @pl.when(owner > me)
            def _():
                col_arrival(owner, feat).wait_recv()

            @pl.when(owner >= me)
            def _():
                col_arrival(owner, other).wait_recv()

        for j in range(GROUP):
            owner = group * GROUP + j
            source = jnp.maximum(owner, me)
            live = jnp.where(feat < counts[owner], 1.0, 0.0)
            rows = jnp.concatenate([emb_ref[row_ids[feat, owner]], rows_sib[owner]], axis=-1)
            rows_wide = rows.astype(jnp.float32)
            scaled = (rows_wide * gain_pair).astype(jnp.bfloat16)
            col = jnp.concatenate([cols[source, feat], cols[source, other]], axis=-1)
            logits = lax.dot_general(
                scaled, col, (((1,), (1,)), ((), ())), preferred_element_type=jnp.float32
            )
            prob = 0.5 * jnp.tanh(0.5 * logits) + 0.5
            residual = ((prob - labels[owner].astype(jnp.float32)) * live).astype(jnp.bfloat16)
            pulled = jnp.dot(residual, col, preferred_element_type=jnp.float32)
            row_term = (pulled * gain_pair).astype(jnp.bfloat16)
            col_term = lax.dot_general(
                residual, scaled, (((0,), (0,)), ((), ())), preferred_element_type=jnp.float32
            ).astype(jnp.bfloat16)
            col_tiles[owner, 0] = col_term[:, :width]
            col_tiles[owner, 1] = col_term[:, width:]
            row_tiles[owner, 0] = row_term[:, :width]
            row_tiles[owner, 1] = row_term[:, width:]
            product = rows_wide * pulled
            gain_sum = gain_sum + jnp.sum(product.reshape(-1, 8, 2 * width), axis=0)

        for j in range(GROUP):
            owner = group * GROUP + j

            @pl.when(owner > me)
            def _():
                back_copy(owner, 0).start()

            @pl.when(owner == me)
            def _():
                back_own().start()

            @pl.when(owner >= me)
            def _():
                back_copy(owner, 1).start()
                row_copy(owner).start()
                row_own(owner).start()

        return gain_sum

    gain_sum = lax.fori_loop(
        first_group, groups, work, jnp.zeros((8, 2 * width), jnp.float32)
    )

    gain_send[0] = gain_sum[:, width:]
    gain_pairwise = remote(
        gain_send.at[0], gain_sib, small_send_sem.at[1], small_recv_sem.at[1], sibling
    )
    gain_pairwise.start()
    gain_pairwise.wait_recv()
    chip_gain = jnp.sum(gain_sum[:, :width] + gain_sib[...], axis=0, keepdims=True)
    chip_gain = jnp.broadcast_to(chip_gain, (8, width))
    gain_send[1] = chip_gain
    gain_all[me] = chip_gain

    def gain_copy(step):
        chip = lax.rem(me + step, owners)
        return remote(
            gain_send.at[1], gain_all.at[me], gain_send_sem.at[chip],
            gain_recv_sem.at[me], device(chip, feat),
        )

    def gain_arrival(step):
        chip = lax.rem(me + step, owners)
        return remote(
            gain_send.at[1], gain_all.at[chip], gain_send_sem.at[chip],
            gain_recv_sem.at[chip], device(chip, feat),
        )

    def start_gain(step, _):
        gain_copy(step).start()
        return 0

    lax.fori_loop(1, owners, start_gain, 0)

    def wait_gain(step, _):
        gain_arrival(step).wait_recv()
        gain_copy(step).wait_send()
        return 0

    lax.fori_loop(1, owners, wait_gain, 0)

    def add_gain(chip, total):
        return total + gain_all[chip]

    total = lax.fori_loop(0, owners, add_gain, jnp.zeros((8, width), jnp.float32))
    gain_out[...] = total * (16.0 / (owners * emb_ref.shape[1]))

    def drain_cols(step, _):
        chip = me - step
        for slot in range(2):
            col_copy(chip, slot).wait_send()
            term_arrival(slot, chip).wait_recv()
        return 0

    lax.fori_loop(1, me + 1, drain_cols, 0)
    col_copy(me, other).wait_send()
    term_arrival(other, me).wait_recv()
    back_own().wait()

    def drain_rows(group, _):
        rows_copy(group).wait_send()
        return 0

    lax.fori_loop(first_group, groups, drain_rows, 0)

    def drain_back(owner, _):
        back_copy(owner, 1).wait_send()
        row_copy(owner).wait_send()
        row_own(owner).wait()
        term_arrival(other, owner + 1).wait_recv()
        return 0

    lax.fori_loop(me, owners, drain_back, 0)

    def drain_back_own(owner, _):
        back_copy(owner, 0).wait_send()
        return 0

    lax.fori_loop(me + 1, owners, drain_back_own, 0)
    gain_scale.wait_send()
    gain_pairwise.wait_send()


def add_kernel(ids, terms_ref, out_ref):
    out_ref[...] = jnp.zeros_like(out_ref)
    places = terms_ref.shape[1]

    def add(place, _):
        for slot in range(2):
            block = ids[slot, place]
            out_ref[block] += terms_ref[slot, place].astype(jnp.float32)
        return 0

    lax.fori_loop(0, places, add, 0)


def local(embeddings, decoder_gain, block_pairs, pair_counts, edge_labels):
    partners = lax.axis_size("partner")
    owners = lax.axis_size("row") * partners
    me = lax.axis_index(("row", "partner"))
    tile = edge_labels.shape[-1]
    width = embeddings.shape[1]
    blocks = embeddings.shape[0] // tile
    resident = embeddings.reshape(blocks, tile, width)
    labels = edge_labels.reshape(owners, 2, tile, tile)
    base = me * blocks
    as_requester = lax.dynamic_index_in_dim(block_pairs, me, 0, keepdims=False)
    as_owner = lax.dynamic_index_in_dim(block_pairs, me, 1, keepdims=False)
    row_ids = (as_requester[:, :, 0] - base).T
    col_ids = (as_owner[:, :, 1] - base).T
    counts = lax.dynamic_index_in_dim(pair_counts, me, 0, keepdims=False)
    place = jnp.arange(owners + 1)[None, :]
    ids = jnp.where(
        place <= me,
        jnp.pad(col_ids, ((0, 0), (0, 1))),
        jnp.pad(row_ids, ((0, 0), (1, 0))),
    )
    gain_rows = jnp.broadcast_to(decoder_gain[None, :], (8, width))

    smem = pl.BlockSpec(memory_space=pltpu.SMEM)
    vmem = pl.BlockSpec(memory_space=pltpu.VMEM)
    anywhere = pl.BlockSpec(memory_space=pl.ANY)
    dma = pltpu.SemaphoreType.DMA
    half = jnp.bfloat16
    groups = owners // GROUP
    terms, gain_total = pl.pallas_call(
        functools.partial(exchange_kernel, owners, partners),
        out_shape=(
            jax.ShapeDtypeStruct((2, owners + 1, tile, width), half),
            jax.ShapeDtypeStruct((8, width), jnp.float32),
        ),
        in_specs=[smem, smem, smem, vmem, vmem, anywhere],
        out_specs=(anywhere, vmem),
        scratch_shapes=[
            pltpu.VMEM((2, owners, tile, width), half),
            pltpu.VMEM((owners, 2, tile, width), half),
            pltpu.VMEM((owners, tile, width), half),
            pltpu.VMEM((owners, tile, width), half),
            pltpu.VMEM((owners, tile, tile), half),
            pltpu.VMEM((owners, 2, tile, width), half),
            pltpu.VMEM((owners, 2, tile, width), half),
            pltpu.VMEM((2, 8, width), jnp.float32),
            pltpu.VMEM((2, 8, width), jnp.float32),
            pltpu.VMEM((8, width), jnp.float32),
            pltpu.VMEM((owners, 8, width), jnp.float32),
            dma((2, owners)),
            dma((owners, 2)),
            dma((groups,)),
            dma((groups,)),
            dma((groups,)),
            dma((owners, 2)),
            dma((owners,)),
            dma((2, owners + 1)),
            dma((owners + 1,)),
            dma((2,)),
            dma((2,)),
            dma((owners,)),
            dma((owners,)),
        ],
        compiler_params=pltpu.CompilerParams(
            has_side_effects=True, vmem_limit_bytes=48 * 2**20
        ),
        name="exchange",
    )(row_ids, col_ids, counts, gain_rows, resident, labels)

    part = tile // NODE_SPLIT
    grad = pl.pallas_call(
        add_kernel,
        grid_spec=pltpu.PrefetchScalarGridSpec(
            num_scalar_prefetch=1,
            grid=(NODE_SPLIT,),
            in_specs=[pl.BlockSpec((2, owners + 1, part, width), lambda i, ids: (0, 0, i, 0))],
            out_specs=pl.BlockSpec((blocks, part, width), lambda i, ids: (0, i, 0)),
        ),
        out_shape=jax.ShapeDtypeStruct((blocks, tile, width), jnp.float32),
        compiler_params=pltpu.CompilerParams(vmem_limit_bytes=48 * 2**20),
        name="add_terms",
    )(ids, terms)
    return grad.reshape(blocks * tile, width), gain_total[0]


def solution(mesh):
    in_specs = (
        P(("row", "partner"), "feat"),
        P("feat"),
        P(),
        P(),
        P(("row", "partner"), None, None, None, None),
    )
    out_specs = (P(("row", "partner"), "feat"), P("feat"))
    return jax.shard_map(local, mesh=mesh, in_specs=in_specs, out_specs=out_specs, check_vma=False)
```

time: 679 us -> 161 us (0.24)
  the two profiles are of different devices: /device:TPU:8 before, /device:TPU:2 now
where the time goes in v1:
time: 161 us; the launch traced here: 159 us
  Pallas kernels  151 us (94%)
  local copies, waits for them, and re-layouts  6.76 us (4%)
    pallas_call x1, Pallas kernels, local(): pl.pallas_call(functools.partial(exchange_kernel, owners, partners), out_...  146 us
    pallas_call x1, Pallas kernels, local(): pl.pallas_call(add_kernel, grid_spec=pltpu.PrefetchScalarGridSpec(num_sca...  5.31 us
    unnamed x6, local copies, waits for them, and re-layouts  4.56 us

profile of v1, /device:TPU:2, one launch (start us, length us, event | category | flops | bytes accessed | tf_op | source)
XLA Modules:
  0.0 158.8 jit_solution(11722848117220767048)
XLA Ops:
  0.6 0.0 copy-start
  0.7 0.7 fusion.counts
  1.4 0.1 copy-done
  1.5 0.7 broadcast_in_dim.16.gain_ref
  2.2 0.2 constant_dynamic-slice_fusion.1
  2.4 0.1 copy.7
  2.5 0.1 pad_select_fusion.ids
  2.6 0.0 copy-start.2
  2.6 2.2 %copy-done.2 = bf16[16384,128]{1,0:T(8,128)(2,1)S(1)} copy-done((bf16[16384,128]{1,0:T(8,128)(2,1)S(1)}, bf16[16384,128]{1,0:T(8,128)(2,1)}, u32[]{:S(2)}) %copy-start.2) | copy-done | bytes 4194328
  4.8 146.0 %exchange.1 = (bf16[2,65,128,128]{3,2,1,0:T(8,128)(2,1)}, f32[8,128]{1,0:T(8,128)S(1)}) custom-call(s32[2,64]{1,0:T(2,128)S(1)} %bitcast.18, s32[2,64]{1,0:T(2,128)S(1)} %bitcast.20, s32[64]{0:T(128)S(1)} %fusion.counts, f32[8,128]{1,0:T(8,128)S(1)} %broadcast_in_dim.16.gain_ref, bf16[128,128,128]{2,1,0:T(8,128)(2,1)S(1)} %bitcast.16, ...), custom_call_target="tpu_custom_call" | custom-call | tf_op jit(solution)/shard_map/exchange/pallas_call | solution.py:338
  150.8 0.5 slice_bitcast_fusion
  151.3 0.0 copy-start.1
  151.3 2.2 %copy-done.1 = bf16[2,65,128,128]{3,2,1,0:T(8,128)(2,1)S(1)} copy-done((bf16[2,65,128,128]{3,2,1,0:T(8,128)(2,1)S(1)}, bf16[2,65,128,128]{3,2,1,0:T(8,128)(2,1)}, u32[]{:S(2)}) %copy-start.1) | copy-done | bytes 4259864
  153.5 5.3 %add_terms.1 = f32[128,128,128]{2,1,0:T(8,128)} custom-call(s32[2,65]{1,0:T(2,128)S(1)} %pad_select_fusion.ids, bf16[2,65,128,128]{3,2,1,0:T(8,128)(2,1)S(1)} %copy-done.1), custom_call_target="tpu_custom_call" | custom-call | tf_op jit(solution)/shard_map/add_terms/pallas_call | solution.py:379
  (3 shorter events, 0.0 us)
Async XLA Ops:
  0.6 0.9 copy-start
  2.6 2.2 %copy-start.2 = (bf16[16384,128]{1,0:T(8,128)(2,1)S(1)}, bf16[16384,128]{1,0:T(8,128)(2,1)}, u32[]{:S(2)}) copy-start(bf16[16384,128]{1,0:T(8,128)(2,1)} %param.5) | copy-start | bytes 12582916
  151.3 2.2 %copy-start.1 = (bf16[2,65,128,128]{3,2,1,0:T(8,128)(2,1)S(1)}, bf16[2,65,128,128]{3,2,1,0:T(8,128)(2,1)}, u32[]{:S(2)}) copy-start(bf16[2,65,128,128]{3,2,1,0:T(8,128)(2,1)} %get-tuple-element.4.terms_ref) | copy-start | bytes 12779524

commit v2 on v0

v2 whole, which is shorter than its diff:
```python
import functools

import jax
import jax.numpy as jnp
from jax import lax
from jax.experimental import pallas as pl
from jax.experimental.pallas import tpu as pltpu
from jax.sharding import PartitionSpec as P

NODE_SPLIT = 2
MESH = pl.DeviceIdType.MESH


def exchange_kernel(
    chips,
    span,
    sent_ids,
    kept_ids,
    diagonal_ids,
    live,
    gain_ref,
    emb_hbm,
    labels_hbm,
    terms_hbm,
    gain_out,
    emb,
    staged,
    staged_sib,
    blocks,
    labels,
    grads,
    gains,
    gain_send,
    gain_sib,
    gain_all,
    emb_sem,
    block_send_sem,
    block_recv_sem,
    label_send_sem,
    label_recv_sem,
    label_own_sem,
    sib_send_sem,
    sib_recv_sem,
    back_send_sem,
    keep_send_sem,
    keep_own_sem,
    term_recv_sem,
    small_send_sem,
    small_recv_sem,
    gain_send_sem,
    gain_recv_sem,
):
    row = lax.axis_index("row")
    x, y, z = row // span, lax.axis_index("partner"), row % span
    me = row * span + y
    feat = lax.axis_index("feat")
    other = 1 - feat
    width = emb.shape[-1]
    half_rows = labels.shape[1] // 2
    my_rows = pl.ds(pl.multiple_of(feat * half_rows, half_rows), half_rows)

    def place(chip, core):
        return (chip // span, chip % span, core)

    sibling = place(me, other)

    def remote(src, dst, send, recv, where):
        return pltpu.make_async_remote_copy(
            src_ref=src, dst_ref=dst, send_sem=send, recv_sem=recv,
            device_id=where, device_id_type=MESH,
        )

    def shifted(step, sign):
        d = step % span
        b = (step // span) % span
        c = step // (span * span)
        dx = (d + b) % span
        px = (x + sign * dx + span) % span
        py = (y + sign * ((d + c) % span) + span) % span
        pz = (z + sign * d + span) % span
        return (px * span + pz) * span + py, dx % 2

    def kept_role(peer):
        return jnp.where(peer < me, 1, 0)

    def block_copy(peer, core):
        role = jnp.where(peer > me, 0, 1)
        return remote(
            staged.at[peer], blocks.at[me, role, feat], block_send_sem.at[peer],
            block_recv_sem.at[me, feat], place(peer, core),
        )

    def block_arrival(peer, half):
        return remote(
            staged.at[peer], blocks.at[peer, 1 - kept_role(peer), half], block_send_sem.at[peer],
            block_recv_sem.at[peer, half], sibling,
        )

    def label_copy(peer, core):
        return remote(
            labels_hbm.at[peer, 1, my_rows], labels.at[me, my_rows], label_send_sem.at[peer],
            label_recv_sem.at[me, feat], place(peer, core),
        )

    def label_arrival(peer, half):
        return remote(
            labels_hbm.at[peer, 1, pl.ds(half * half_rows, half_rows)],
            labels.at[peer, pl.ds(half * half_rows, half_rows)],
            label_send_sem.at[peer], label_recv_sem.at[peer, half], sibling,
        )

    def label_own(peer, slot):
        return pltpu.make_async_copy(
            labels_hbm.at[peer, slot], labels.at[peer], label_own_sem.at[peer]
        )

    def sib_copy(peer):
        return remote(
            staged_sib.at[peer], blocks.at[peer, kept_role(peer), feat], sib_send_sem.at[peer],
            sib_recv_sem.at[peer], sibling,
        )

    def sib_arrival(peer):
        return remote(
            staged_sib.at[peer], blocks.at[peer, kept_role(peer), other], sib_send_sem.at[peer],
            sib_recv_sem.at[peer], sibling,
        )

    def diagonal_col_copy():
        return remote(
            staged.at[me], blocks.at[me, 1, feat], block_send_sem.at[me],
            block_recv_sem.at[me, feat], sibling,
        )

    def diagonal_col_arrival():
        return remote(
            staged.at[me], blocks.at[me, 1, other], block_send_sem.at[me],
            block_recv_sem.at[me, other], sibling,
        )

    def back_copy(peer, half):
        return remote(
            grads.at[peer, 1 - kept_role(peer), half], terms_hbm.at[0, me],
            back_send_sem.at[peer, half], term_recv_sem.at[0, me], place(peer, half),
        )

    def keep_copy(peer):
        return remote(
            grads.at[peer, kept_role(peer), other], terms_hbm.at[1, peer],
            keep_send_sem.at[peer], term_recv_sem.at[1, peer], sibling,
        )

    def keep_own(peer):
        return pltpu.make_async_copy(
            grads.at[peer, kept_role(peer), feat], terms_hbm.at[1, peer], keep_own_sem.at[peer]
        )

    def diagonal_copy(role):
        where = me if role == 0 else chips
        return remote(
            grads.at[me, role, other], terms_hbm.at[feat, where],
            back_send_sem.at[me, role], term_recv_sem.at[feat, where], sibling,
        )

    def diagonal_own(role):
        where = me if role == 0 else chips
        return pltpu.make_async_copy(
            grads.at[me, role, feat], terms_hbm.at[feat, where], keep_own_sem.at[chips - role * chips + role * me]
        )

    def term_arrival(kind, where):
        return remote(
            staged.at[0], terms_hbm.at[kind, where], keep_send_sem.at[0],
            term_recv_sem.at[kind, where], sibling,
        )

    emb_copy = pltpu.make_async_copy(emb_hbm, emb, emb_sem.at[0])
    emb_copy.start()
    barrier = pltpu.get_barrier_semaphore()
    pl.semaphore_signal(barrier, 1, device_id=sibling, device_id_type=MESH)

    def greet(step, _):
        peer = lax.rem(me + step, chips)
        for core in range(2):
            pl.semaphore_signal(barrier, 1, device_id=place(peer, core), device_id_type=MESH)
        return 0

    lax.fori_loop(1, chips, greet, 0)
    label_own(me, feat).start()

    def load_labels(step, _):
        peer, core = shifted(step, -1)

        @pl.when((core == feat) & (peer > me))
        def _():
            label_own(peer, 0).start()

        return 0

    lax.fori_loop(1, chips, load_labels, 0)
    emb_copy.wait()

    def stage(step, _):
        peer, core = shifted(step, 1)
        staged[peer] = emb[sent_ids[peer]]

        @pl.when(core == feat)
        def _():
            blocks[peer, kept_role(peer), feat] = emb[kept_ids[peer]]

        @pl.when(core == other)
        def _():
            staged_sib[peer] = emb[kept_ids[peer]]

        return 0

    lax.fori_loop(1, chips, stage, 0)
    staged_sib[me] = emb[diagonal_ids[other, 0]]
    staged[me] = emb[diagonal_ids[other, 1]]
    blocks[me, 0, feat] = emb[diagonal_ids[feat, 0]]
    blocks[me, 1, feat] = emb[diagonal_ids[feat, 1]]
    gains[feat] = gain_ref[...]

    pl.semaphore_wait(barrier, 2 * chips - 1)
    gain_scale = remote(
        gain_ref, gains.at[feat], small_send_sem.at[0], small_recv_sem.at[0], sibling
    )
    gain_scale.start()
    sib_copy(me).start()
    diagonal_col_copy().start()

    def send(step, _):
        peer, core = shifted(step, 1)
        block_copy(peer, core).start()

        @pl.when(peer > me)
        def _():
            label_copy(peer, core).start()

        mirror, core_mirror = shifted(step, -1)

        @pl.when(core_mirror == other)
        def _():
            sib_copy(mirror).start()

        return 0

    lax.fori_loop(1, chips, send, 0)

    gain_scale.wait_recv()
    gain_pair = jnp.concatenate([gains[feat], gains[other]], axis=-1)[:1]

    def tile(peer, goes_to, is_live, gain_sum):
        rows = jnp.concatenate([blocks[peer, 0, feat], blocks[peer, 0, other]], axis=-1)
        col = jnp.concatenate([blocks[peer, 1, feat], blocks[peer, 1, other]], axis=-1)
        rows_wide = rows.astype(jnp.float32)
        scaled = (rows_wide * gain_pair).astype(jnp.bfloat16)
        logits = lax.dot_general(
            scaled, col, (((1,), (1,)), ((), ())), preferred_element_type=jnp.float32
        )
        prob = 0.5 * jnp.tanh(0.5 * logits) + 0.5
        residual = ((prob - labels[peer].astype(jnp.float32)) * is_live).astype(jnp.bfloat16)
        pulled = jnp.dot(residual, col, preferred_element_type=jnp.float32)
        row_term = (pulled * gain_pair).astype(jnp.bfloat16)
        col_term = lax.dot_general(
            residual, scaled, (((0,), (0,)), ((), ())), preferred_element_type=jnp.float32
        ).astype(jnp.bfloat16)
        grads[goes_to, 0, feat] = row_term[:, :width]
        grads[goes_to, 0, other] = row_term[:, width:]
        grads[goes_to, 1, feat] = col_term[:, :width]
        grads[goes_to, 1, other] = col_term[:, width:]
        product = rows_wide * pulled
        return gain_sum + jnp.sum(product.reshape(-1, 8, 2 * width), axis=0)

    sib_arrival(me).wait_recv()
    diagonal_col_arrival().wait_recv()
    label_own(me, feat).wait()
    gain_sum = tile(
        me, me, jnp.where(live[me] > feat, 1.0, 0.0), jnp.zeros((8, 2 * width), jnp.float32)
    )
    for role in range(2):
        diagonal_copy(role).start()
        diagonal_own(role).start()

    def mine(group, j):
        window = 2 * group + j // (span // 2)
        d = (feat + window) % 2 + 2 * (j % (span // 2))
        return shifted(window * span + d, -1)[0]

    def work(group, gain_sum):
        peers = [mine(group, j) for j in range(span)]
        for peer in peers:

            @pl.when(peer != me)
            def _(peer=peer):
                sib_arrival(peer).wait_recv()
                for half in range(2):
                    block_arrival(peer, half).wait_recv()

            @pl.when(peer > me)
            def _(peer=peer):
                label_own(peer, 0).wait()

            @pl.when(peer < me)
            def _(peer=peer):
                for half in range(2):
                    label_arrival(peer, half).wait_recv()

        for peer in peers:
            is_live = jnp.where(live[peer] > 0, 1.0, 0.0)
            is_live = jnp.where(peer == me, 0.0, is_live)
            gain_sum = tile(peer, jnp.where(peer == me, chips, peer), is_live, gain_sum)
        for peer in peers:

            @pl.when(peer != me)
            def _(peer=peer):
                for half in range(2):
                    back_copy(peer, half).start()
                keep_copy(peer).start()
                keep_own(peer).start()

        return gain_sum

    gain_sum = lax.fori_loop(0, chips // (2 * span), work, gain_sum)

    gain_send[0] = gain_sum[:, width:]
    gain_pairwise = remote(
        gain_send.at[0], gain_sib, small_send_sem.at[1], small_recv_sem.at[1], sibling
    )
    gain_pairwise.start()
    gain_pairwise.wait_recv()
    chip_gain = jnp.sum(gain_sum[:, :width] + gain_sib[...], axis=0, keepdims=True)
    chip_gain = jnp.broadcast_to(chip_gain, (8, width))
    gain_send[1] = chip_gain
    gain_all[me] = chip_gain

    def gain_copy(peer):
        return remote(
            gain_send.at[1], gain_all.at[me], gain_send_sem.at[peer],
            gain_recv_sem.at[me], place(peer, feat),
        )

    def gain_arrival(peer):
        return remote(
            gain_send.at[1], gain_all.at[peer], gain_send_sem.at[peer],
            gain_recv_sem.at[peer], sibling,
        )

    def start_gain(step, _):
        gain_copy(shifted(step, 1)[0]).start()
        return 0

    lax.fori_loop(1, chips, start_gain, 0)

    def drain(step, _):
        peer, core = shifted(step, 1)
        block_copy(peer, core).wait_send()

        @pl.when(peer > me)
        def _():
            label_copy(peer, core).wait_send()

        term_arrival(0, peer).wait_recv()

        @pl.when(core == other)
        def _():
            sib_copy(peer).wait_send()
            term_arrival(1, peer).wait_recv()

        @pl.when(core == feat)
        def _():
            for half in range(2):
                back_copy(peer, half).wait_send()
            keep_copy(peer).wait_send()
            keep_own(peer).wait()

        return 0

    lax.fori_loop(1, chips, drain, 0)

    def wait_gain(step, _):
        peer = shifted(step, 1)[0]
        gain_arrival(peer).wait_recv()
        gain_copy(peer).wait_send()
        return 0

    lax.fori_loop(1, chips, wait_gain, 0)

    def add_gain(chip, total):
        return total + gain_all[chip]

    total = lax.fori_loop(0, chips, add_gain, jnp.zeros((8, width), jnp.float32))
    gain_out[...] = total * (16.0 / (chips * emb.shape[1]))

    for role in range(2):
        diagonal_copy(role).wait_send()
        diagonal_own(role).wait()
        term_arrival(other, me if role == 0 else chips).wait_recv()
    sib_copy(me).wait_send()
    diagonal_col_copy().wait_send()
    gain_scale.wait_send()
    gain_pairwise.wait_send()


def add_kernel(ids, terms_ref, out_ref):
    out_ref[...] = jnp.zeros_like(out_ref)
    places = terms_ref.shape[1]

    def add(where, _):
        for slot in range(2):
            block = ids[slot, where]
            out_ref[block] += terms_ref[slot, where].astype(jnp.float32)
        return 0

    lax.fori_loop(0, places, add, 0)


def local(embeddings, decoder_gain, block_pairs, pair_counts, edge_labels):
    span = lax.axis_size("partner")
    chips = lax.axis_size("row") * span
    me = lax.axis_index(("row", "partner"))
    tile = edge_labels.shape[-1]
    width = embeddings.shape[1]
    count = embeddings.shape[0] // tile
    resident = embeddings.reshape(count, tile, width)
    labels = edge_labels.reshape(chips, 2, tile, tile)
    base = me * count
    row_ids = lax.dynamic_index_in_dim(block_pairs, me, 0, keepdims=False)[:, :, 0] - base
    col_ids = lax.dynamic_index_in_dim(block_pairs, me, 1, keepdims=False)[:, :, 1] - base
    as_requester = lax.dynamic_index_in_dim(pair_counts, me, 0, keepdims=False)
    as_owner = lax.dynamic_index_in_dim(pair_counts, me, 1, keepdims=False)
    peers = jnp.arange(chips)
    sent_ids = jnp.where(peers > me, row_ids[:, 1], col_ids[:, 0])
    kept_ids = jnp.where(peers > me, row_ids[:, 0], col_ids[:, 1])
    live = jnp.where(peers < me, as_owner - 1, as_requester)
    diagonal_ids = jnp.stack(
        [
            lax.dynamic_index_in_dim(row_ids, me, 0, keepdims=False),
            lax.dynamic_index_in_dim(col_ids, me, 0, keepdims=False),
        ],
        axis=1,
    )
    ids = jnp.where(peers == me, diagonal_ids[:, :1], jnp.stack([sent_ids, kept_ids]))
    ids = jnp.concatenate([ids, diagonal_ids[:, 1:]], axis=1)
    gain_rows = jnp.broadcast_to(decoder_gain[None, :], (8, width))

    smem = pl.BlockSpec(memory_space=pltpu.SMEM)
    vmem = pl.BlockSpec(memory_space=pltpu.VMEM)
    anywhere = pl.BlockSpec(memory_space=pl.ANY)
    dma = pltpu.SemaphoreType.DMA
    half = jnp.bfloat16
    terms, gain_total = pl.pallas_call(
        functools.partial(exchange_kernel, chips, span),
        out_shape=(
            jax.ShapeDtypeStruct((2, chips + 1, tile, width), half),
            jax.ShapeDtypeStruct((8, width), jnp.float32),
        ),
        in_specs=[smem, smem, smem, smem, vmem, anywhere, anywhere],
        out_specs=(anywhere, vmem),
        scratch_shapes=[
            pltpu.VMEM((count, tile, width), half),
            pltpu.VMEM((chips, tile, width), half),
            pltpu.VMEM((chips, tile, width), half),
            pltpu.VMEM((chips, 2, 2, tile, width), half),
            pltpu.VMEM((chips, tile, tile), half),
            pltpu.VMEM((chips + 1, 2, 2, tile, width), half),
            pltpu.VMEM((2, 8, width), jnp.float32),
            pltpu.VMEM((2, 8, width), jnp.float32),
            pltpu.VMEM((8, width), jnp.float32),
            pltpu.VMEM((chips, 8, width), jnp.float32),
            dma((1,)),
            dma((chips,)),
            dma((chips, 2)),
            dma((chips,)),
            dma((chips, 2)),
            dma((chips,)),
            dma((chips,)),
            dma((chips,)),
            dma((chips, 2)),
            dma((chips,)),
            dma((chips + 1,)),
            dma((2, chips + 1)),
            dma((2,)),
            dma((2,)),
            dma((chips,)),
            dma((chips,)),
        ],
        compiler_params=pltpu.CompilerParams(
            collective_id=0, has_side_effects=True, vmem_limit_bytes=56 * 2**20
        ),
        name="exchange",
    )(sent_ids, kept_ids, diagonal_ids, live, gain_rows, resident, labels)

    part = tile // NODE_SPLIT
    grad = pl.pallas_call(
        add_kernel,
        grid_spec=pltpu.PrefetchScalarGridSpec(
            num_scalar_prefetch=1,
            grid=(NODE_SPLIT,),
            in_specs=[pl.BlockSpec((2, chips + 1, part, width), lambda i, ids: (0, 0, i, 0))],
            out_specs=pl.BlockSpec((count, part, width), lambda i, ids: (0, i, 0)),
        ),
        out_shape=jax.ShapeDtypeStruct((count, tile, width), jnp.float32),
        compiler_params=pltpu.CompilerParams(vmem_limit_bytes=48 * 2**20),
        name="add_terms",
    )(ids, terms)
    return grad.reshape(count * tile, width), gain_total[0]


def solution(mesh):
    in_specs = (
        P(("row", "partner"), "feat"),
        P("feat"),
        P(),
        P(),
        P(("row", "partner"), None, None, None, None),
    )
    out_specs = (P(("row", "partner"), "feat"), P("feat"))
    return jax.shard_map(local, mesh=mesh, in_specs=in_specs, out_specs=out_specs, check_vma=False)
```

time: 679 us -> 103 us (0.15)
  the two profiles are of different devices: /device:TPU:8 before, /device:TPU:7 now
where the time goes in v2:
time: 103 us
  Pallas kernels  94 us (91%)
  local copies, waits for them, and re-layouts  5.15 us (5%)
  other arithmetic  3.03 us (3%)
    pallas_call x1, Pallas kernels, local(): pl.pallas_call(functools.partial(exchange_kernel, chips, span), out_shape...  88.7 us
    pallas_call x1, Pallas kernels, local(): pl.pallas_call(add_kernel, grid_spec=pltpu.PrefetchScalarGridSpec(num_sca...  5.31 us
    unnamed x4, local copies, waits for them, and re-layouts  2.22 us

profile of v2, /device:TPU:7, one launch (start us, length us, event | category | flops | bytes accessed | tf_op | source)
XLA Modules:
  0.0 102.9 jit_solution(16989473441887946732)
XLA Ops:
  0.6 0.0 copy-start
  0.7 1.0 add_reduce_fusion
  1.6 0.0 copy-done
  1.7 1.3 %broadcast_in_dim.23.gain_ref = f32[8,128]{1,0:T(8,128)} broadcast(f32[128]{0:T(128)} %param.6), dimensions={1} | broadcast | bytes 4608 | tf_op jit(solution)/shard_map/broadcast_in_dim | solution.py:445
  2.9 0.2 constant_dynamic-slice_fusion.2
  3.1 0.1 copy.16
  3.2 1.3 %compare_select_fusion.1 = (s32[64]{0:T(128)}, s32[64]{0:T(128)}, s32[64]{0:T(128)}) fusion(s32[64,2]{0,1:T(2,128)S(1)} %bitcast.37, s32[64,2]{0,1:T(2,128)S(1)} %bitcast.35, s32[]{:T(128)S(6)} %add.18, s32[64]{0:T(128)S(1)} %add_reduce_fusion, s32[64,64]{1,0:T(8,128)} %param.8, s32[]{:T(128)S(6)} %select_n.31), kind=kLoop, calls=%fused_computation.7 | loop fusion | flops 320 | bytes 2312 | tf_op jit(solution)/shard_map/jit(_where)/select_n | solution.py:434
  4.5 0.2 fusion.1
  4.7 0.1 add_select_fusion
  4.8 0.1 pad_add_fusion.ids
  4.9 0.6 pad_add_fusion.1.diagonal_ids
  5.5 88.7 %exchange.1 = (bf16[2,65,128,128]{3,2,1,0:T(8,128)(2,1)}, f32[8,128]{1,0:T(8,128)}) custom-call(s32[64]{0:T(128)} %get-tuple-element.9.sent_ids, s32[64]{0:T(128)} %get-tuple-element.8.kept_ids, s32[2,2]{1,0:T(2,128)} %pad_add_fusion.1.diagonal_ids, s32[64]{0:T(128)} %get-tuple-element.12.live, f32[8,128]{1,0:T(8,128)} %broadcast_in_dim.23.gain_ref, ...), custom_call_target="tpu_custom_call" | custom-call | tf_op jit(solution)/shard_map/exchange/pallas_call | solution.py:452
  94.2 1.2 %slice_bitcast_fusion = f32[128]{0:T(128)} fusion(f32[8,128]{1,0:T(8,128)} %get-tuple-element.5), kind=kLoop, calls=%fused_computation.17 | loop fusion | bytes 1024 | tf_op jit(solution)/shard_map/squeeze | solution.py:507
  95.4 0.0 copy-start.1
  95.4 2.2 %copy-done.1 = bf16[2,65,128,128]{3,2,1,0:T(8,128)(2,1)S(1)} copy-done((bf16[2,65,128,128]{3,2,1,0:T(8,128)(2,1)S(1)}, bf16[2,65,128,128]{3,2,1,0:T(8,128)(2,1)}, u32[]{:S(2)}) %copy-start.1) | copy-done | bytes 4259864
  97.6 5.3 %add_terms.1 = f32[128,128,128]{2,1,0:T(8,128)} custom-call(s32[2,65]{1,0:T(2,128)S(1)} %pad_add_fusion.ids, bf16[2,65,128,128]{3,2,1,0:T(8,128)(2,1)S(1)} %copy-done.1), custom_call_target="tpu_custom_call" | custom-call | tf_op jit(solution)/shard_map/add_terms/pallas_call | solution.py:495
  (5 shorter events, 0.0 us)
Async XLA Ops:
  0.6 1.0 copy-start
  95.4 2.2 %copy-start.1 = (bf16[2,65,128,128]{3,2,1,0:T(8,128)(2,1)S(1)}, bf16[2,65,128,128]{3,2,1,0:T(8,128)(2,1)}, u32[]{:S(2)}) copy-start(bf16[2,65,128,128]{3,2,1,0:T(8,128)(2,1)} %get-tuple-element.4.terms_ref) | copy-start | bytes 12779524

commit v3 on v2

--- a/solution.py
+++ b/solution.py
@@ -14,15 +14,16 @@
 def exchange_kernel(
     chips,
     span,
-    sent_ids,
-    kept_ids,
-    diagonal_ids,
-    live,
     gain_ref,
+    pairs_hbm,
+    counts_hbm,
     emb_hbm,
     labels_hbm,
     terms_hbm,
     gain_out,
+    ids_out,
+    pairs,
+    counts,
     emb,
     staged,
     staged_sib,
@@ -33,7 +34,7 @@
     gain_send,
     gain_sib,
     gain_all,
-    emb_sem,
+    entry_sem,
     block_send_sem,
     block_recv_sem,
     label_send_sem,
@@ -70,15 +71,28 @@
             device_id=where, device_id_type=MESH,
         )
 
-    def shifted(step, sign):
-        d = step % span
-        b = (step // span) % span
-        c = step // (span * span)
-        dx = (d + b) % span
-        px = (x + sign * dx + span) % span
-        py = (y + sign * ((d + c) % span) + span) % span
-        pz = (z + sign * d + span) % span
-        return (px * span + pz) * span + py, dx % 2
+    count = emb.shape[0]
+    base = me * count
+
+    def resident(block):
+        return jnp.clip(block - base, 0, count - 1)
+
+    def sent_id(peer):
+        return resident(jnp.where(peer > me, pairs[me, 1, 0, peer], pairs[peer, 0, 1, me]))
+
+    def kept_id(peer):
+        return resident(jnp.where(peer > me, pairs[me, 0, 0, peer], pairs[peer, 1, 1, me]))
+
+    def diagonal_id(slot, role):
+        return resident(pairs[me, slot, role, me])
+
+    def window_step(window, d, sign):
+        b, c = lax.rem(window, span), lax.div(window, span)
+        dx, dy = lax.rem(d + b, span), lax.rem(d + c, span)
+        if sign < 0:
+            dx, dy, d = span - dx, span - dy, span - d
+        px, py, pz = lax.rem(x + dx, span), lax.rem(y + dy, span), lax.rem(z + d, span)
+        return (px * span + pz) * span + py, lax.rem(dx, 2)
 
     def kept_role(peer):
         return jnp.where(peer < me, 1, 0)
@@ -174,81 +188,102 @@
             term_recv_sem.at[kind, where], sibling,
         )
 
-    emb_copy = pltpu.make_async_copy(emb_hbm, emb, emb_sem.at[0])
+    def each_peer(action, sign):
+        def body(window, _):
+            for d in range(span):
+                peer, core = window_step(window, d, sign)
+                if d == 0:
+                    pl.when(peer != me)(functools.partial(action, peer, core))
+                else:
+                    action(peer, core)
+            return 0
+
+        lax.fori_loop(0, span * span, body, 0)
+
+    emb_copy = pltpu.make_async_copy(emb_hbm, emb, entry_sem.at[0])
+    pairs_copy = pltpu.make_async_copy(pairs_hbm, pairs, entry_sem.at[1])
+    counts_copy = pltpu.make_async_copy(counts_hbm, counts, entry_sem.at[2])
+    pairs_copy.start()
     emb_copy.start()
+    counts_copy.start()
     barrier = pltpu.get_barrier_semaphore()
     pl.semaphore_signal(barrier, 1, device_id=sibling, device_id_type=MESH)
 
-    def greet(step, _):
-        peer = lax.rem(me + step, chips)
+    def greet(peer, core):
         for core in range(2):
             pl.semaphore_signal(barrier, 1, device_id=place(peer, core), device_id_type=MESH)
+
+    each_peer(greet, 1)
+    gains[feat] = gain_ref[...]
+    pairs_copy.wait()
+    emb_copy.wait()
+
+    def stage(step, _):
+        for j in range(4):
+            peer = step * 4 + j
+            staged[peer] = emb[sent_id(peer)]
         return 0
 
-    lax.fori_loop(1, chips, greet, 0)
-    label_own(me, feat).start()
-
-    def load_labels(step, _):
-        peer, core = shifted(step, -1)
-
-        @pl.when((core == feat) & (peer > me))
-        def _():
-            label_own(peer, 0).start()
-
-        return 0
-
-    lax.fori_loop(1, chips, load_labels, 0)
-    emb_copy.wait()
-
-    def stage(step, _):
-        peer, core = shifted(step, 1)
-        staged[peer] = emb[sent_ids[peer]]
-
-        @pl.when(core == feat)
-        def _():
-            blocks[peer, kept_role(peer), feat] = emb[kept_ids[peer]]
-
-        @pl.when(core == other)
-        def _():
-            staged_sib[peer] = emb[kept_ids[peer]]
-
-        return 0
-
-    lax.fori_loop(1, chips, stage, 0)
-    staged_sib[me] = emb[diagonal_ids[other, 0]]
-    staged[me] = emb[diagonal_ids[other, 1]]
-    blocks[me, 0, feat] = emb[diagonal_ids[feat, 0]]
-    blocks[me, 1, feat] = emb[diagonal_ids[feat, 1]]
-    gains[feat] = gain_ref[...]
+    lax.fori_loop(0, chips // 4, stage, 0)
+    staged_sib[me] = emb[diagonal_id(other, 0)]
+    staged[me] = emb[diagonal_id(other, 1)]
 
     pl.semaphore_wait(barrier, 2 * chips - 1)
     gain_scale = remote(
         gain_ref, gains.at[feat], small_send_sem.at[0], small_recv_sem.at[0], sibling
     )
+
+    def send(peer, core):
+        block_copy(peer, core).start()
+
+        @pl.when(peer > me)
+        def _():
+            label_copy(peer, core).start()
+
+    each_peer(send, 1)
+
     gain_scale.start()
     sib_copy(me).start()
     diagonal_col_copy().start()
-
-    def send(step, _):
-        peer, core = shifted(step, 1)
-        block_copy(peer, core).start()
-
-        @pl.when(peer > me)
+    label_own(me, feat).start()
+    blocks[me, 0, feat] = emb[diagonal_id(feat, 0)]
+    blocks[me, 1, feat] = emb[diagonal_id(feat, 1)]
+
+    def keep(peer, core):
+        @pl.when(core == other)
         def _():
-            label_copy(peer, core).start()
-
-        mirror, core_mirror = shifted(step, -1)
-
-        @pl.when(core_mirror == other)
+            staged_sib[peer] = emb[kept_id(peer)]
+            sib_copy(peer).start()
+
+        @pl.when(core == feat)
         def _():
-            sib_copy(mirror).start()
-
+            blocks[peer, kept_role(peer), feat] = emb[kept_id(peer)]
+
+            @pl.when(peer > me)
+            def _():
+                label_own(peer, 0).start()
+
+    each_peer(keep, -1)
+
+    def list_ids(peer, _):
+        on_diagonal = peer == me
+        ids_out[0, peer] = jnp.where(on_diagonal, diagonal_id(0, 0), sent_id(peer))
+        ids_out[1, peer] = jnp.where(on_diagonal, diagonal_id(1, 0), kept_id(peer))
         return 0
 
-    lax.fori_loop(1, chips, send, 0)
+    lax.fori_loop(0, chips, list_ids, 0)
+    for slot in range(2):
+        ids_out[slot, chips] = diagonal_id(slot, 1)
+    counts_copy.wait()
+
+    def live(peer):
+        at_requester = jnp.where(counts[me, peer] > 0, 1.0, 0.0)
+        at_owner = jnp.where(counts[peer, me] > 1, 1.0, 0.0)
+        worked = jnp.where(peer > me, at_requester, at_owner)
+        return jnp.where(peer == me, 0.0, worked)
 
     gain_scale.wait_recv()
-    gain_pair = jnp.concatenate([gains[feat], gains[other]], axis=-1)[:1]
+    gain_pair = jnp.concatenate([gains[feat], gains[other]], axis=-1)
 
     def tile(peer, goes_to, is_live, gain_sum):
         rows = jnp.concatenate([blocks[peer, 0, feat], blocks[peer, 0, other]], axis=-1)
@@ -276,7 +311,7 @@
     diagonal_col_arrival().wait_recv()
     label_own(me, feat).wait()
     gain_sum = tile(
-        me, me, jnp.where(live[me] > feat, 1.0, 0.0), jnp.zeros((8, 2 * width), jnp.float32)
+        me, me, jnp.where(counts[me, me] > feat, 1.0, 0.0), jnp.zeros((8, 2 * width), jnp.float32)
     )
     for role in range(2):
         diagonal_copy(role).start()
@@ -284,8 +319,8 @@
 
     def mine(group, j):
         window = 2 * group + j // (span // 2)
-        d = (feat + window) % 2 + 2 * (j % (span // 2))
-        return shifted(window * span + d, -1)[0]
+        d = lax.rem(feat + window, 2) + 2 * (j % (span // 2))
+        return window_step(window, d, -1)[0]
 
     def work(group, gain_sum):
         peers = [mine(group, j) for j in range(span)]
@@ -307,9 +342,7 @@
                     label_arrival(peer, half).wait_recv()
 
         for peer in peers:
-            is_live = jnp.where(live[peer] > 0, 1.0, 0.0)
-            is_live = jnp.where(peer == me, 0.0, is_live)
-            gain_sum = tile(peer, jnp.where(peer == me, chips, peer), is_live, gain_sum)
+            gain_sum = tile(peer, jnp.where(peer == me, chips, peer), live(peer), gain_sum)
         for peer in peers:
 
             @pl.when(peer != me)
@@ -323,14 +356,14 @@
 
     gain_sum = lax.fori_loop(0, chips // (2 * span), work, gain_sum)
 
+    gain_sum = jnp.sum(gain_sum, axis=0, keepdims=True)
     gain_send[0] = gain_sum[:, width:]
     gain_pairwise = remote(
         gain_send.at[0], gain_sib, small_send_sem.at[1], small_recv_sem.at[1], sibling
     )
     gain_pairwise.start()
     gain_pairwise.wait_recv()
-    chip_gain = jnp.sum(gain_sum[:, :width] + gain_sib[...], axis=0, keepdims=True)
-    chip_gain = jnp.broadcast_to(chip_gain, (8, width))
+    chip_gain = gain_sum[:, :width] + gain_sib[...]
     gain_send[1] = chip_gain
     gain_all[me] = chip_gain
 
@@ -346,14 +379,9 @@
             gain_recv_sem.at[peer], sibling,
         )
 
-    def start_gain(step, _):
-        gain_copy(shifted(step, 1)[0]).start()
-        return 0
-
-    lax.fori_loop(1, chips, start_gain, 0)
-
-    def drain(step, _):
-        peer, core = shifted(step, 1)
+    each_peer(lambda peer, core: gain_copy(peer).start(), 1)
+
+    def drain(peer, core):
         block_copy(peer, core).wait_send()
 
         @pl.when(peer > me)
@@ -374,22 +402,18 @@
             keep_copy(peer).wait_send()
             keep_own(peer).wait()
 
-        return 0
-
-    lax.fori_loop(1, chips, drain, 0)
-
-    def wait_gain(step, _):
-        peer = shifted(step, 1)[0]
+    each_peer(drain, 1)
+
+    def wait_gain(peer, core):
         gain_arrival(peer).wait_recv()
         gain_copy(peer).wait_send()
-        return 0
-
-    lax.fori_loop(1, chips, wait_gain, 0)
+
+    each_peer(wait_gain, 1)
 
     def add_gain(chip, total):
         return total + gain_all[chip]
 
-    total = lax.fori_loop(0, chips, add_gain, jnp.zeros((8, width), jnp.float32))
+    total = lax.fori_loop(0, chips, add_gain, jnp.zeros((1, width), jnp.float32))
     gain_out[...] = total * (16.0 / (chips * emb.shape[1]))
 
     for role in range(2):
@@ -402,7 +426,8 @@
     gain_pairwise.wait_send()
 
 
-def add_kernel(ids, terms_ref, out_ref):
+def add_kernel(ids, terms_ref, gain_ref, out_ref, gain_out):
+    gain_out[...] = gain_ref[...]
     out_ref[...] = jnp.zeros_like(out_ref)
     places = terms_ref.shape[1]
 
@@ -418,57 +443,41 @@
 def local(embeddings, decoder_gain, block_pairs, pair_counts, edge_labels):
     span = lax.axis_size("partner")
     chips = lax.axis_size("row") * span
-    me = lax.axis_index(("row", "partner"))
     tile = edge_labels.shape[-1]
     width = embeddings.shape[1]
     count = embeddings.shape[0] // tile
     resident = embeddings.reshape(count, tile, width)
     labels = edge_labels.reshape(chips, 2, tile, tile)
-    base = me * count
-    row_ids = lax.dynamic_index_in_dim(block_pairs, me, 0, keepdims=False)[:, :, 0] - base
-    col_ids = lax.dynamic_index_in_dim(block_pairs, me, 1, keepdims=False)[:, :, 1] - base
-    as_requester = lax.dynamic_index_in_dim(pair_counts, me, 0, keepdims=False)
-    as_owner = lax.dynamic_index_in_dim(pair_counts, me, 1, keepdims=False)
-    peers = jnp.arange(chips)
-    sent_ids = jnp.where(peers > me, row_ids[:, 1], col_ids[:, 0])
-    kept_ids = jnp.where(peers > me, row_ids[:, 0], col_ids[:, 1])
-    live = jnp.where(peers < me, as_owner - 1, as_requester)
-    diagonal_ids = jnp.stack(
-        [
-            lax.dynamic_index_in_dim(row_ids, me, 0, keepdims=False),
-            lax.dynamic_index_in_dim(col_ids, me, 0, keepdims=False),
-        ],
-        axis=1,
-    )
-    ids = jnp.where(peers == me, diagonal_ids[:, :1], jnp.stack([sent_ids, kept_ids]))
-    ids = jnp.concatenate([ids, diagonal_ids[:, 1:]], axis=1)
-    gain_rows = jnp.broadcast_to(decoder_gain[None, :], (8, width))
+    pairs = block_pairs.transpose(0, 2, 3, 1)
 
     smem = pl.BlockSpec(memory_space=pltpu.SMEM)
     vmem = pl.BlockSpec(memory_space=pltpu.VMEM)
     anywhere = pl.BlockSpec(memory_space=pl.ANY)
     dma = pltpu.SemaphoreType.DMA
     half = jnp.bfloat16
-    terms, gain_total = pl.pallas_call(
+    terms, gain_total, ids = pl.pallas_call(
         functools.partial(exchange_kernel, chips, span),
         out_shape=(
             jax.ShapeDtypeStruct((2, chips + 1, tile, width), half),
-            jax.ShapeDtypeStruct((8, width), jnp.float32),
+            jax.ShapeDtypeStruct((1, width), jnp.float32),
+            jax.ShapeDtypeStruct((2, chips + 1), jnp.int32),
         ),
-        in_specs=[smem, smem, smem, smem, vmem, anywhere, anywhere],
-        out_specs=(anywhere, vmem),
+        in_specs=[vmem, anywhere, anywhere, anywhere, anywhere],
+        out_specs=(anywhere, vmem, smem),
         scratch_shapes=[
+            pltpu.SMEM((chips, 2, 2, chips), jnp.int32),
+            pltpu.SMEM((chips, chips), jnp.int32),
             pltpu.VMEM((count, tile, width), half),
             pltpu.VMEM((chips, tile, width), half),
             pltpu.VMEM((chips, tile, width), half),
             pltpu.VMEM((chips, 2, 2, tile, width), half),
             pltpu.VMEM((chips, tile, tile), half),
             pltpu.VMEM((chips + 1, 2, 2, tile, width), half),
-            pltpu.VMEM((2, 8, width), jnp.float32),
-            pltpu.VMEM((2, 8, width), jnp.float32),
-            pltpu.VMEM((8, width), jnp.float32),
-            pltpu.VMEM((chips, 8, width), jnp.float32),
-            dma((1,)),
+            pltpu.VMEM((2, 1, width), jnp.float32),
+            pltpu.VMEM((2, 1, width), jnp.float32),
+            pltpu.VMEM((1, width), jnp.float32),
+            pltpu.VMEM((chips, 1, width), jnp.float32),
+            dma((3,)),
             dma((chips,)),
             dma((chips, 2)),
             dma((chips,)),
@@ -489,22 +498,31 @@
             collective_id=0, has_side_effects=True, vmem_limit_bytes=56 * 2**20
         ),
         name="exchange",
-    )(sent_ids, kept_ids, diagonal_ids, live, gain_rows, resident, labels)
+    )(decoder_gain.reshape(1, width), pairs, pair_counts, resident, labels)
 
     part = tile // NODE_SPLIT
-    grad = pl.pallas_call(
+    grad, gain = pl.pallas_call(
         add_kernel,
         grid_spec=pltpu.PrefetchScalarGridSpec(
             num_scalar_prefetch=1,
             grid=(NODE_SPLIT,),
-            in_specs=[pl.BlockSpec((2, chips + 1, part, width), lambda i, ids: (0, 0, i, 0))],
-            out_specs=pl.BlockSpec((count, part, width), lambda i, ids: (0, i, 0)),
+            in_specs=[
+                pl.BlockSpec((2, chips + 1, part, width), lambda i, ids: (0, 0, i, 0)),
+                pl.BlockSpec((1, width), lambda i, ids: (0, 0)),
+            ],
+            out_specs=(
+                pl.BlockSpec((count, part, width), lambda i, ids: (0, i, 0)),
+                pl.BlockSpec((1, width), lambda i, ids: (0, 0)),
+            ),
         ),
-        out_shape=jax.ShapeDtypeStruct((count, tile, width), jnp.float32),
-        compiler_params=pltpu.CompilerParams(vmem_limit_bytes=48 * 2**20),
+        out_shape=(
+            jax.ShapeDtypeStruct((count, tile, width), jnp.float32),
+            jax.ShapeDtypeStruct((1, width), jnp.float32),
+        ),
+        compiler_params=pltpu.CompilerParams(vmem_limit_bytes=60 * 2**20),
         name="add_terms",
-    )(ids, terms)
-    return grad.reshape(count * tile, width), gain_total[0]
+    )(ids, terms, gain_total)
+    return grad.reshape(count * tile, width), gain.reshape(width)
 
 
 def solution(mesh):

time: 103 us -> 92.8 us (0.901)
  the two profiles are of different devices: /device:TPU:7 before, /device:TPU:2 now
where the time goes in v3:
time: 92.8 us; the launch traced here: 92.6 us
  Pallas kernels  92 us (99%)
    pallas_call x1, Pallas kernels, local(): pl.pallas_call(functools.partial(exchange_kernel, chips, span), out_shape...  85.2 us
    pallas_call x1, Pallas kernels, local(): pl.pallas_call(add_kernel, grid_spec=pltpu.PrefetchScalarGridSpec(num_sca...  6.78 us

profile of v3, /device:TPU:2, one launch (start us, length us, event | category | flops | bytes accessed | tf_op | source)
XLA Modules:
  0.0 92.6 jit_solution(2452172077042049044)
XLA Ops:
  0.6 85.2 %exchange.1 = (bf16[2,65,128,128]{3,2,1,0:T(8,128)(2,1)}, f32[1,128]{1,0:T(1,128)}, s32[2,65]{1,0:T(2,128)}) custom-call(f32[1,128]{1,0:T(1,128)} %bitcast.9, s32[64,2,2,64]{3,2,1,0:T(2,128)} %bitcast.8, s32[64,64]{1,0:T(8,128)} %counts_hbm.1, bf16[128,128,128]{2,1,0:T(8,128)(2,1)} %bitcast.6, bf16[64,2,128,128]{3,2,1,0:T(8,128)(2,1)} %bitcast.7), custom_call_target="tpu_custom_call" | custom-call | tf_op jit(solution)/shard_map/exchange/pallas_call | solution.py:458
  85.8 6.8 %add_terms.1 = (f32[128,128,128]{2,1,0:T(8,128)}, f32[1,128]{1,0:T(1,128)}) custom-call(s32[2,65]{1,0:T(2,128)} %get-tuple-element.7.ids, bf16[2,65,128,128]{3,2,1,0:T(8,128)(2,1)} %get-tuple-element.8.terms_ref, f32[1,128]{1,0:T(1,128)} %get-tuple-element.9.gain_ref), custom_call_target="tpu_custom_call" | custom-call | tf_op jit(solution)/shard_map/add_terms/pallas_call | solution.py:504

commit v4 on v3

--- a/solution.py
+++ b/solution.py
@@ -35,21 +35,11 @@
     gain_sib,
     gain_all,
     entry_sem,
-    block_send_sem,
-    block_recv_sem,
+    arrive_sem,
     label_send_sem,
-    label_recv_sem,
-    label_own_sem,
-    sib_send_sem,
-    sib_recv_sem,
-    back_send_sem,
-    keep_send_sem,
-    keep_own_sem,
-    term_recv_sem,
-    small_send_sem,
-    small_recv_sem,
-    gain_send_sem,
-    gain_recv_sem,
+    send_sem,
+    term_sem,
+    small_sem,
 ):
     row = lax.axis_index("row")
     x, y, z = row // span, lax.axis_index("partner"), row % span
@@ -94,98 +84,74 @@
         px, py, pz = lax.rem(x + dx, span), lax.rem(y + dy, span), lax.rem(z + d, span)
         return (px * span + pz) * span + py, lax.rem(dx, 2)
 
+    groups = chips // (2 * span)
+    block_sends, sib_sends, back_sends, diagonal_sends, gain_sends = (
+        send_sem.at[k] for k in range(5)
+    )
+
+    def wait_bytes(ref, sem):
+        pltpu.make_async_copy(ref, ref, sem).wait()
+
+    def group_of(window):
+        return arrive_sem.at[lax.div(window, 2)]
+
     def kept_role(peer):
         return jnp.where(peer < me, 1, 0)
 
-    def block_copy(peer, core):
+    def block_copy(peer, core, window):
         role = jnp.where(peer > me, 0, 1)
         return remote(
-            staged.at[peer], blocks.at[me, role, feat], block_send_sem.at[peer],
-            block_recv_sem.at[me, feat], place(peer, core),
-        )
-
-    def block_arrival(peer, half):
-        return remote(
-            staged.at[peer], blocks.at[peer, 1 - kept_role(peer), half], block_send_sem.at[peer],
-            block_recv_sem.at[peer, half], sibling,
-        )
-
-    def label_copy(peer, core):
+            staged.at[peer], blocks.at[me, role, feat], block_sends, group_of(window),
+            place(peer, core),
+        )
+
+    def label_copy(peer, core, window):
         return remote(
             labels_hbm.at[peer, 1, my_rows], labels.at[me, my_rows], label_send_sem.at[peer],
-            label_recv_sem.at[me, feat], place(peer, core),
-        )
-
-    def label_arrival(peer, half):
-        return remote(
-            labels_hbm.at[peer, 1, pl.ds(half * half_rows, half_rows)],
-            labels.at[peer, pl.ds(half * half_rows, half_rows)],
-            label_send_sem.at[peer], label_recv_sem.at[peer, half], sibling,
-        )
-
-    def label_own(peer, slot):
-        return pltpu.make_async_copy(
-            labels_hbm.at[peer, slot], labels.at[peer], label_own_sem.at[peer]
-        )
-
-    def sib_copy(peer):
-        return remote(
-            staged_sib.at[peer], blocks.at[peer, kept_role(peer), feat], sib_send_sem.at[peer],
-            sib_recv_sem.at[peer], sibling,
-        )
-
-    def sib_arrival(peer):
-        return remote(
-            staged_sib.at[peer], blocks.at[peer, kept_role(peer), other], sib_send_sem.at[peer],
-            sib_recv_sem.at[peer], sibling,
+            group_of(window), place(peer, core),
+        )
+
+    def label_own(peer, slot, sem):
+        return pltpu.make_async_copy(labels_hbm.at[peer, slot], labels.at[peer], sem)
+
+    def sib_copy(peer, sem):
+        return remote(
+            staged_sib.at[peer], blocks.at[peer, kept_role(peer), feat], sib_sends, sem, sibling
         )
 
     def diagonal_col_copy():
         return remote(
-            staged.at[me], blocks.at[me, 1, feat], block_send_sem.at[me],
-            block_recv_sem.at[me, feat], sibling,
-        )
-
-    def diagonal_col_arrival():
-        return remote(
-            staged.at[me], blocks.at[me, 1, other], block_send_sem.at[me],
-            block_recv_sem.at[me, other], sibling,
+            staged.at[me], blocks.at[me, 1, feat], block_sends, arrive_sem.at[groups], sibling
         )
 
     def back_copy(peer, half):
         return remote(
-            grads.at[peer, 1 - kept_role(peer), half], terms_hbm.at[0, me],
-            back_send_sem.at[peer, half], term_recv_sem.at[0, me], place(peer, half),
+            grads.at[peer, 1 - kept_role(peer), half], terms_hbm.at[0, me], back_sends,
+            term_sem.at[0], place(peer, half),
         )
 
     def keep_copy(peer):
         return remote(
-            grads.at[peer, kept_role(peer), other], terms_hbm.at[1, peer],
-            keep_send_sem.at[peer], term_recv_sem.at[1, peer], sibling,
+            grads.at[peer, kept_role(peer), other], terms_hbm.at[1, peer], sib_sends,
+            term_sem.at[1], sibling,
         )
 
     def keep_own(peer):
         return pltpu.make_async_copy(
-            grads.at[peer, kept_role(peer), feat], terms_hbm.at[1, peer], keep_own_sem.at[peer]
+            grads.at[peer, kept_role(peer), feat], terms_hbm.at[1, peer], term_sem.at[1]
         )
 
     def diagonal_copy(role):
         where = me if role == 0 else chips
         return remote(
-            grads.at[me, role, other], terms_hbm.at[feat, where],
-            back_send_sem.at[me, role], term_recv_sem.at[feat, where], sibling,
+            grads.at[me, role, other], terms_hbm.at[feat, where], diagonal_sends,
+            term_sem.at[0], sibling,
         )
 
     def diagonal_own(role):
         where = me if role == 0 else chips
         return pltpu.make_async_copy(
-            grads.at[me, role, feat], terms_hbm.at[feat, where], keep_own_sem.at[chips - role * chips + role * me]
-        )
-
-    def term_arrival(kind, where):
-        return remote(
-            staged.at[0], terms_hbm.at[kind, where], keep_send_sem.at[0],
-            term_recv_sem.at[kind, where], sibling,
+            grads.at[me, role, feat], terms_hbm.at[feat, where], term_sem.at[1]
         )
 
     def each_peer(action, sign):
@@ -193,9 +159,9 @@
             for d in range(span):
                 peer, core = window_step(window, d, sign)
                 if d == 0:
-                    pl.when(peer != me)(functools.partial(action, peer, core))
+                    pl.when(peer != me)(functools.partial(action, peer, core, window))
                 else:
-                    action(peer, core)
+                    action(peer, core, window)
             return 0
 
         lax.fori_loop(0, span * span, body, 0)
@@ -209,7 +175,7 @@
     barrier = pltpu.get_barrier_semaphore()
     pl.semaphore_signal(barrier, 1, device_id=sibling, device_id_type=MESH)
 
-    def greet(peer, core):
+    def greet(peer, core, window):
         for core in range(2):
             pl.semaphore_signal(barrier, 1, device_id=place(peer, core), device_id_type=MESH)
 
@@ -230,30 +196,30 @@
 
     pl.semaphore_wait(barrier, 2 * chips - 1)
     gain_scale = remote(
-        gain_ref, gains.at[feat], small_send_sem.at[0], small_recv_sem.at[0], sibling
+        gain_ref, gains.at[feat], small_sem.at[0], small_sem.at[1], sibling
     )
 
-    def send(peer, core):
-        block_copy(peer, core).start()
+    def send(peer, core, window):
+        block_copy(peer, core, window).start()
 
         @pl.when(peer > me)
         def _():
-            label_copy(peer, core).start()
+            label_copy(peer, core, window).start()
 
     each_peer(send, 1)
 
     gain_scale.start()
-    sib_copy(me).start()
+    sib_copy(me, arrive_sem.at[groups]).start()
     diagonal_col_copy().start()
-    label_own(me, feat).start()
+    label_own(me, feat, arrive_sem.at[groups]).start()
     blocks[me, 0, feat] = emb[diagonal_id(feat, 0)]
     blocks[me, 1, feat] = emb[diagonal_id(feat, 1)]
 
-    def keep(peer, core):
+    def keep(peer, core, window):
         @pl.when(core == other)
         def _():
             staged_sib[peer] = emb[kept_id(peer)]
-            sib_copy(peer).start()
+            sib_copy(peer, group_of(window)).start()
 
         @pl.when(core == feat)
         def _():
@@ -261,7 +227,7 @@
 
             @pl.when(peer > me)
             def _():
-                label_own(peer, 0).start()
+                label_own(peer, 0, group_of(window)).start()
 
     each_peer(keep, -1)
 
@@ -307,9 +273,7 @@
         product = rows_wide * pulled
         return gain_sum + jnp.sum(product.reshape(-1, 8, 2 * width), axis=0)
 
-    sib_arrival(me).wait_recv()
-    diagonal_col_arrival().wait_recv()
-    label_own(me, feat).wait()
+    wait_bytes(staged.at[pl.ds(0, 3)], arrive_sem.at[groups])
     gain_sum = tile(
         me, me, jnp.where(counts[me, me] > feat, 1.0, 0.0), jnp.zeros((8, 2 * width), jnp.float32)
     )
@@ -324,22 +288,15 @@
 
     def work(group, gain_sum):
         peers = [mine(group, j) for j in range(span)]
-        for peer in peers:
-
-            @pl.when(peer != me)
-            def _(peer=peer):
-                sib_arrival(peer).wait_recv()
-                for half in range(2):
-                    block_arrival(peer, half).wait_recv()
-
-            @pl.when(peer > me)
-            def _(peer=peer):
-                label_own(peer, 0).wait()
-
-            @pl.when(peer < me)
-            def _(peer=peer):
-                for half in range(2):
-                    label_arrival(peer, half).wait_recv()
+        short = (group == 0) & (feat == 0)
+
+        @pl.when(short)
+        def _():
+            wait_bytes(blocks.at[pl.ds(0, span - 1)], arrive_sem.at[0])
+
+        @pl.when(jnp.logical_not(short))
+        def _():
+            wait_bytes(blocks.at[pl.ds(0, span)], arrive_sem.at[group])
 
         for peer in peers:
             gain_sum = tile(peer, jnp.where(peer == me, chips, peer), live(peer), gain_sum)
@@ -354,12 +311,12 @@
 
         return gain_sum
 
-    gain_sum = lax.fori_loop(0, chips // (2 * span), work, gain_sum)
+    gain_sum = lax.fori_loop(0, groups, work, gain_sum)
 
     gain_sum = jnp.sum(gain_sum, axis=0, keepdims=True)
     gain_send[0] = gain_sum[:, width:]
     gain_pairwise = remote(
-        gain_send.at[0], gain_sib, small_send_sem.at[1], small_recv_sem.at[1], sibling
+        gain_send.at[0], gain_sib, small_sem.at[2], small_sem.at[3], sibling
     )
     gain_pairwise.start()
     gain_pairwise.wait_recv()
@@ -367,48 +324,35 @@
     gain_send[1] = chip_gain
     gain_all[me] = chip_gain
 
-    def gain_copy(peer):
-        return remote(
-            gain_send.at[1], gain_all.at[me], gain_send_sem.at[peer],
-            gain_recv_sem.at[me], place(peer, feat),
-        )
-
-    def gain_arrival(peer):
-        return remote(
-            gain_send.at[1], gain_all.at[peer], gain_send_sem.at[peer],
-            gain_recv_sem.at[peer], sibling,
-        )
-
-    each_peer(lambda peer, core: gain_copy(peer).start(), 1)
-
-    def drain(peer, core):
-        block_copy(peer, core).wait_send()
-
+    def start_gain(peer, core, window):
+        remote(
+            gain_send.at[1], gain_all.at[me], gain_sends, small_sem.at[4], place(peer, feat)
+        ).start()
+
+    each_peer(start_gain, 1)
+
+    wait_bytes(terms_hbm.at[1], term_sem.at[1])
+    wait_bytes(staged, block_sends)
+    wait_bytes(staged, sib_sends)
+    wait_bytes(grads.at[0, 0], diagonal_sends)
+    half_peers = chips // 2
+
+    @pl.when(feat == 0)
+    def _():
+        wait_bytes(grads.at[pl.ds(0, half_peers - 1), 0], back_sends)
+
+    @pl.when(feat == 1)
+    def _():
+        wait_bytes(grads.at[pl.ds(0, half_peers), 0], back_sends)
+
+    def drain_label(peer, core, window):
         @pl.when(peer > me)
         def _():
-            label_copy(peer, core).wait_send()
-
-        term_arrival(0, peer).wait_recv()
-
-        @pl.when(core == other)
-        def _():
-            sib_copy(peer).wait_send()
-            term_arrival(1, peer).wait_recv()
-
-        @pl.when(core == feat)
-        def _():
-            for half in range(2):
-                back_copy(peer, half).wait_send()
-            keep_copy(peer).wait_send()
-            keep_own(peer).wait()
-
-    each_peer(drain, 1)
-
-    def wait_gain(peer, core):
-        gain_arrival(peer).wait_recv()
-        gain_copy(peer).wait_send()
-
-    each_peer(wait_gain, 1)
+            label_copy(peer, core, window).wait_send()
+
+    each_peer(drain_label, 1)
+    wait_bytes(gain_all.at[pl.ds(0, chips - 1)], gain_sends)
+    wait_bytes(gain_all.at[pl.ds(0, chips - 1)], small_sem.at[4])
 
     def add_gain(chip, total):
         return total + gain_all[chip]
@@ -416,12 +360,7 @@
     total = lax.fori_loop(0, chips, add_gain, jnp.zeros((1, width), jnp.float32))
     gain_out[...] = total * (16.0 / (chips * emb.shape[1]))
 
-    for role in range(2):
-        diagonal_copy(role).wait_send()
-        diagonal_own(role).wait()
-        term_arrival(other, me if role == 0 else chips).wait_recv()
-    sib_copy(me).wait_send()
-    diagonal_col_copy().wait_send()
+    wait_bytes(terms_hbm.at[0], term_sem.at[0])
     gain_scale.wait_send()
     gain_pairwise.wait_send()
 
@@ -478,21 +417,11 @@
             pltpu.VMEM((1, width), jnp.float32),
             pltpu.VMEM((chips, 1, width), jnp.float32),
             dma((3,)),
+            dma((chips // (2 * span) + 1,)),
             dma((chips,)),
-            dma((chips, 2)),
-            dma((chips,)),
-            dma((chips, 2)),
-            dma((chips,)),
-            dma((chips,)),
-            dma((chips,)),
-            dma((chips, 2)),
-            dma((chips,)),
-            dma((chips + 1,)),
-            dma((2, chips + 1)),
+            dma((5,)),
             dma((2,)),
-            dma((2,)),
-            dma((chips,)),
-            dma((chips,)),
+            dma((5,)),
         ],
         compiler_params=pltpu.CompilerParams(
             collective_id=0, has_side_effects=True, vmem_limit_bytes=56 * 2**20

time: 92.8 us -> 83.2 us (0.90)
  Pallas kernels: 92 us -> 82.4 us
    pallas_call x1, Pallas kernels: 85.2 us -> 75.6 us  [local(): pl.pallas_call(functools.partial(exchange_kernel, chips, span), out_shape...]
where the time goes in v4:
time: 83.2 us; the launch traced here: 83 us
  Pallas kernels  82.4 us (99%)
    pallas_call x1, Pallas kernels, local(): pl.pallas_call(functools.partial(exchange_kernel, chips, span), out_shape...  75.6 us
    pallas_call x1, Pallas kernels, local(): pl.pallas_call(add_kernel, grid_spec=pltpu.PrefetchScalarGridSpec(num_sca...  6.78 us

profile of v4, /device:TPU:2, one launch (start us, length us, event | category | flops | bytes accessed | tf_op | source)
XLA Modules:
  0.0 83.0 jit_solution(17202689313281170179)
XLA Ops:
  0.6 75.6 %exchange.1 = (bf16[2,65,128,128]{3,2,1,0:T(8,128)(2,1)}, f32[1,128]{1,0:T(1,128)}, s32[2,65]{1,0:T(2,128)}) custom-call(f32[1,128]{1,0:T(1,128)} %bitcast.9, s32[64,2,2,64]{3,2,1,0:T(2,128)} %bitcast.8, s32[64,64]{1,0:T(8,128)} %counts_hbm.1, bf16[128,128,128]{2,1,0:T(8,128)(2,1)} %bitcast.6, bf16[64,2,128,128]{3,2,1,0:T(8,128)(2,1)} %bitcast.7), custom_call_target="tpu_custom_call" | custom-call | tf_op jit(solution)/shard_map/exchange/pallas_call | solution.py:397
  76.2 6.8 %add_terms.1 = (f32[128,128,128]{2,1,0:T(8,128)}, f32[1,128]{1,0:T(1,128)}) custom-call(s32[2,65]{1,0:T(2,128)} %get-tuple-element.7.ids, bf16[2,65,128,128]{3,2,1,0:T(8,128)(2,1)} %get-tuple-element.8.terms_ref, f32[1,128]{1,0:T(1,128)} %get-tuple-element.9.gain_ref), custom_call_target="tpu_custom_call" | custom-call | tf_op jit(solution)/shard_map/add_terms/pallas_call | solution.py:433

commit v5 on v4

--- a/solution.py
+++ b/solution.py
@@ -7,7 +7,7 @@
 from jax.experimental.pallas import tpu as pltpu
 from jax.sharding import PartitionSpec as P
 
-NODE_SPLIT = 2
+PIECES = 8
 MESH = pl.DeviceIdType.MESH
 
 
@@ -19,7 +19,7 @@
     counts_hbm,
     emb_hbm,
     labels_hbm,
-    terms_hbm,
+    terms,
     gain_out,
     ids_out,
     pairs,
@@ -85,6 +85,7 @@
         return (px * span + pz) * span + py, lax.rem(dx, 2)
 
     groups = chips // (2 * span)
+    places = chips + 1
     block_sends, sib_sends, back_sends, diagonal_sends, gain_sends = (
         send_sem.at[k] for k in range(5)
     )
@@ -126,32 +127,32 @@
 
     def back_copy(peer, half):
         return remote(
-            grads.at[peer, 1 - kept_role(peer), half], terms_hbm.at[0, me], back_sends,
+            grads.at[peer, 1 - kept_role(peer), half], terms.at[me], back_sends,
             term_sem.at[0], place(peer, half),
         )
 
     def keep_copy(peer):
         return remote(
-            grads.at[peer, kept_role(peer), other], terms_hbm.at[1, peer], sib_sends,
+            grads.at[peer, kept_role(peer), other], terms.at[places + peer], sib_sends,
             term_sem.at[1], sibling,
         )
 
     def keep_own(peer):
         return pltpu.make_async_copy(
-            grads.at[peer, kept_role(peer), feat], terms_hbm.at[1, peer], term_sem.at[1]
+            grads.at[peer, kept_role(peer), feat], terms.at[places + peer], term_sem.at[1]
         )
 
     def diagonal_copy(role):
         where = me if role == 0 else chips
         return remote(
-            grads.at[me, role, other], terms_hbm.at[feat, where], diagonal_sends,
+            grads.at[me, role, other], terms.at[feat * places + where], diagonal_sends,
             term_sem.at[0], sibling,
         )
 
     def diagonal_own(role):
         where = me if role == 0 else chips
         return pltpu.make_async_copy(
-            grads.at[me, role, feat], terms_hbm.at[feat, where], term_sem.at[1]
+            grads.at[me, role, feat], terms.at[feat * places + where], term_sem.at[1]
         )
 
     def each_peer(action, sign):
@@ -331,7 +332,7 @@
 
     each_peer(start_gain, 1)
 
-    wait_bytes(terms_hbm.at[1], term_sem.at[1])
+    wait_bytes(terms.at[pl.ds(places, places)], term_sem.at[1])
     wait_bytes(staged, block_sends)
     wait_bytes(staged, sib_sends)
     wait_bytes(grads.at[0, 0], diagonal_sends)
@@ -360,23 +361,77 @@
     total = lax.fori_loop(0, chips, add_gain, jnp.zeros((1, width), jnp.float32))
     gain_out[...] = total * (16.0 / (chips * emb.shape[1]))
 
-    wait_bytes(terms_hbm.at[0], term_sem.at[0])
+    wait_bytes(terms.at[pl.ds(0, places)], term_sem.at[0])
     gain_scale.wait_send()
     gain_pairwise.wait_send()
 
 
-def add_kernel(ids, terms_ref, gain_ref, out_ref, gain_out):
+def add_kernel(ids, terms, gain_ref, out_hbm, gain_out, sums, head, following, out_sem):
+    none = terms.shape[0]
+    places = none // 2
+    count = sums.shape[0]
+    piece = count // PIECES
+
+    def copy_out(k):
+        span = pl.ds(k * piece, piece)
+        return pltpu.make_async_copy(sums.at[span], out_hbm.at[span], out_sem.at[k])
+
     gain_out[...] = gain_ref[...]
-    out_ref[...] = jnp.zeros_like(out_ref)
-    places = terms_ref.shape[1]
-
-    def add(where, _):
+    following[none] = none
+
+    def clear(step, _):
+        for j in range(4):
+            head[step * 4 + j] = none
+        return 0
+
+    lax.fori_loop(0, count // 4, clear, 0)
+
+    def link(place, _):
         for slot in range(2):
-            block = ids[slot, where]
-            out_ref[block] += terms_ref[slot, where].astype(jnp.float32)
-        return 0
-
-    lax.fori_loop(0, places, add, 0)
+            term = slot * places + place
+            block = ids[slot, place]
+            following[term] = head[block]
+            head[block] = term
+        return 0
+
+    lax.fori_loop(0, places, link, 0)
+
+    def term_or_zero(t):
+        return jnp.where(t < none, terms[jnp.minimum(t, none - 1)].astype(jnp.float32), 0.0)
+
+    def four(step, _):
+        blocks = [step * 4 + j for j in range(4)]
+        first = [head[b] for b in blocks]
+        second = [following[t] for t in first]
+        third = [following[t] for t in second]
+        for b, t, u in zip(blocks, first, second):
+            sums[b] = term_or_zero(t) + term_or_zero(u)
+        least = jnp.minimum(jnp.minimum(third[0], third[1]), jnp.minimum(third[2], third[3]))
+
+        @pl.when(least < none)
+        def _():
+            for b, t in zip(blocks, third):
+
+                def rest(t, b=b):
+                    sums[b] += terms[t].astype(jnp.float32)
+                    return following[t]
+
+                lax.while_loop(lambda t: t < none, rest, t)
+
+        return 0
+
+    def one_piece(k, _):
+        lax.fori_loop(k * (piece // 4), (k + 1) * (piece // 4), four, 0)
+        copy_out(k).start()
+        return 0
+
+    lax.fori_loop(0, PIECES, one_piece, 0)
+
+    def finish(k, _):
+        copy_out(k).wait()
+        return 0
+
+    lax.fori_loop(0, PIECES, finish, 0)
 
 
 def local(embeddings, decoder_gain, block_pairs, pair_counts, edge_labels):
@@ -397,12 +452,12 @@
     terms, gain_total, ids = pl.pallas_call(
         functools.partial(exchange_kernel, chips, span),
         out_shape=(
-            jax.ShapeDtypeStruct((2, chips + 1, tile, width), half),
-            jax.ShapeDtypeStruct((1, width), jnp.float32),
-            jax.ShapeDtypeStruct((2, chips + 1), jnp.int32),
+            pltpu.VMEM((2 * (chips + 1), tile, width), half),
+            pltpu.VMEM((1, width), jnp.float32),
+            pltpu.SMEM((2, chips + 1), jnp.int32),
         ),
         in_specs=[vmem, anywhere, anywhere, anywhere, anywhere],
-        out_specs=(anywhere, vmem, smem),
+        out_specs=(vmem, vmem, smem),
         scratch_shapes=[
             pltpu.SMEM((chips, 2, 2, chips), jnp.int32),
             pltpu.SMEM((chips, chips), jnp.int32),
@@ -427,30 +482,36 @@
             collective_id=0, has_side_effects=True, vmem_limit_bytes=56 * 2**20
         ),
         name="exchange",
-    )(decoder_gain.reshape(1, width), pairs, pair_counts, resident, labels)
-
-    part = tile // NODE_SPLIT
+    )(
+        decoder_gain.reshape(1, width),
+        *(
+            pltpu.with_memory_space_constraint(array, pltpu.HBM)
+            for array in (pairs, pair_counts, resident, labels)
+        ),
+    )
+
+    places = 2 * (chips + 1)
     grad, gain = pl.pallas_call(
         add_kernel,
-        grid_spec=pltpu.PrefetchScalarGridSpec(
-            num_scalar_prefetch=1,
-            grid=(NODE_SPLIT,),
-            in_specs=[
-                pl.BlockSpec((2, chips + 1, part, width), lambda i, ids: (0, 0, i, 0)),
-                pl.BlockSpec((1, width), lambda i, ids: (0, 0)),
-            ],
-            out_specs=(
-                pl.BlockSpec((count, part, width), lambda i, ids: (0, i, 0)),
-                pl.BlockSpec((1, width), lambda i, ids: (0, 0)),
-            ),
-        ),
+        in_specs=[smem, vmem, vmem],
+        out_specs=(anywhere, vmem),
         out_shape=(
             jax.ShapeDtypeStruct((count, tile, width), jnp.float32),
             jax.ShapeDtypeStruct((1, width), jnp.float32),
         ),
-        compiler_params=pltpu.CompilerParams(vmem_limit_bytes=60 * 2**20),
+        scratch_shapes=[
+            pltpu.VMEM((count, tile, width), jnp.float32),
+            pltpu.SMEM((count,), jnp.int32),
+            pltpu.SMEM((places + 1,), jnp.int32),
+            dma((PIECES,)),
+        ],
+        compiler_params=pltpu.CompilerParams(vmem_limit_bytes=48 * 2**20),
         name="add_terms",
-    )(ids, terms, gain_total)
+    )(
+        pltpu.with_memory_space_constraint(ids, pltpu.SMEM),
+        pltpu.with_memory_space_constraint(terms, pltpu.VMEM),
+        pltpu.with_memory_space_constraint(gain_total, pltpu.VMEM),
+    )
     return grad.reshape(count * tile, width), gain.reshape(width)
 
 

time: 83.2 us -> 80.9 us (0.972)
  Pallas kernels: 82.4 us -> 80.1 us
    pallas_call x1, Pallas kernels: 6.78 us -> 5.04 us  [local(): pl.pallas_call(add_kernel, in_specs=[smem, vmem, vmem], out_specs=(anywhe...]
where the time goes in v5:
time: 80.9 us; the launch traced here: 80.7 us
  Pallas kernels  80.1 us (99%)
    pallas_call x1, Pallas kernels, local(): pl.pallas_call(functools.partial(exchange_kernel, chips, span), out_shape...  75.1 us
    pallas_call x1, Pallas kernels, local(): pl.pallas_call(add_kernel, in_specs=[smem, vmem, vmem], out_specs=(anywhe...  5.04 us

profile of v5, /device:TPU:2, one launch (start us, length us, event | category | flops | bytes accessed | tf_op | source)
XLA Modules:
  0.0 80.7 jit_solution(7276359438560982586)
XLA Ops:
  0.6 75.1 %exchange.1 = (bf16[130,128,128]{2,1,0:T(8,128)(2,1)S(1)}, f32[1,128]{1,0:T(1,128)S(1)}, s32[2,65]{1,0:T(2,128)S(4)}) custom-call(f32[1,128]{1,0:T(1,128)} %bitcast.9, s32[64,2,2,64]{3,2,1,0:T(2,128)} %bitcast.8, s32[64,64]{1,0:T(8,128)} %counts_hbm.1, bf16[128,128,128]{2,1,0:T(8,128)(2,1)} %bitcast.6, bf16[64,2,128,128]{3,2,1,0:T(8,128)(2,1)} %bitcast.7), custom_call_target="tpu_custom_call" | custom-call | tf_op jit(solution)/shard_map/exchange/pallas_call | solution.py:452
  75.7 5.0 %add_terms.1 = (f32[128,128,128]{2,1,0:T(8,128)}, f32[1,128]{1,0:T(1,128)}) custom-call(s32[2,65]{1,0:T(2,128)S(4)} %get-tuple-element.7.ids, bf16[130,128,128]{2,1,0:T(8,128)(2,1)S(1)} %get-tuple-element.8.terms, f32[1,128]{1,0:T(1,128)S(1)} %get-tuple-element.9.gain_ref), custom_call_target="tpu_custom_call" | custom-call | tf_op jit(solution)/shard_map/add_terms/pallas_call | solution.py:494

commit v6 on v5

--- a/solution.py
+++ b/solution.py
@@ -185,13 +185,6 @@
     pairs_copy.wait()
     emb_copy.wait()
 
-    def stage(step, _):
-        for j in range(4):
-            peer = step * 4 + j
-            staged[peer] = emb[sent_id(peer)]
-        return 0
-
-    lax.fori_loop(0, chips // 4, stage, 0)
     staged_sib[me] = emb[diagonal_id(other, 0)]
     staged[me] = emb[diagonal_id(other, 1)]
 
@@ -201,6 +194,7 @@
     )
 
     def send(peer, core, window):
+        staged[peer] = emb[sent_id(peer)]
         block_copy(peer, core, window).start()
 
         @pl.when(peer > me)

time: 80.9 us -> 80.6 us (level)
  no operation moved by 1% of the time
where the time goes in v6:
time: 80.6 us; the launch traced here: 80.5 us
  Pallas kernels  79.9 us (99%)
    pallas_call x1, Pallas kernels, local(): pl.pallas_call(functools.partial(exchange_kernel, chips, span), out_shape...  74.8 us
    pallas_call x1, Pallas kernels, local(): pl.pallas_call(add_kernel, in_specs=[smem, vmem, vmem], out_specs=(anywhe...  5.06 us

profile of v6, /device:TPU:2, one launch (start us, length us, event | category | flops | bytes accessed | tf_op | source)
XLA Modules:
  0.0 80.5 jit_solution(7332670426504347077)
XLA Ops:
  0.6 74.8 %exchange.1 = (bf16[130,128,128]{2,1,0:T(8,128)(2,1)S(1)}, f32[1,128]{1,0:T(1,128)S(1)}, s32[2,65]{1,0:T(2,128)S(4)}) custom-call(f32[1,128]{1,0:T(1,128)} %bitcast.9, s32[64,2,2,64]{3,2,1,0:T(2,128)} %bitcast.8, s32[64,64]{1,0:T(8,128)} %counts_hbm.1, bf16[128,128,128]{2,1,0:T(8,128)(2,1)} %bitcast.6, bf16[64,2,128,128]{3,2,1,0:T(8,128)(2,1)} %bitcast.7), custom_call_target="tpu_custom_call" | custom-call | tf_op jit(solution)/shard_map/exchange/pallas_call | solution.py:446
  75.5 5.1 %add_terms.1 = (f32[128,128,128]{2,1,0:T(8,128)}, f32[1,128]{1,0:T(1,128)}) custom-call(s32[2,65]{1,0:T(2,128)S(4)} %get-tuple-element.7.ids, bf16[130,128,128]{2,1,0:T(8,128)(2,1)S(1)} %get-tuple-element.8.terms, f32[1,128]{1,0:T(1,128)S(1)} %get-tuple-element.9.gain_ref), custom_call_target="tpu_custom_call" | custom-call | tf_op jit(solution)/shard_map/add_terms/pallas_call | solution.py:488

commit v7 on v6

--- a/solution.py
+++ b/solution.py
@@ -295,7 +295,10 @@
 
         for peer in peers:
             gain_sum = tile(peer, jnp.where(peer == me, chips, peer), live(peer), gain_sum)
-        for peer in peers:
+        return gain_sum
+
+    def give_back(group):
+        for peer in [mine(group, j) for j in range(span)]:
 
             @pl.when(peer != me)
             def _(peer=peer):
@@ -304,9 +307,14 @@
                 keep_copy(peer).start()
                 keep_own(peer).start()
 
+    def work_and_give(group, gain_sum):
+        gain_sum = work(group, gain_sum)
+        give_back(group)
         return gain_sum
 
-    gain_sum = lax.fori_loop(0, groups, work, gain_sum)
+    last = jnp.int32(groups - 1)
+    gain_sum = lax.fori_loop(0, groups - 1, work_and_give, gain_sum)
+    gain_sum = work(last, gain_sum)
 
     gain_sum = jnp.sum(gain_sum, axis=0, keepdims=True)
     gain_send[0] = gain_sum[:, width:]
@@ -314,6 +322,7 @@
         gain_send.at[0], gain_sib, small_sem.at[2], small_sem.at[3], sibling
     )
     gain_pairwise.start()
+    give_back(last)
     gain_pairwise.wait_recv()
     chip_gain = gain_sum[:, :width] + gain_sib[...]
     gain_send[1] = chip_gain
@@ -380,15 +389,19 @@
 
     lax.fori_loop(0, count // 4, clear, 0)
 
-    def link(place, _):
-        for slot in range(2):
-            term = slot * places + place
-            block = ids[slot, place]
-            following[term] = head[block]
-            head[block] = term
+    unroll = 5 if places % 5 == 0 else 1
+
+    def link(step, _):
+        for j in range(unroll):
+            place = step * unroll + j
+            for slot in range(2):
+                term = slot * places + place
+                block = ids[slot, place]
+                following[term] = head[block]
+                head[block] = term
         return 0
 
-    lax.fori_loop(0, places, link, 0)
+    lax.fori_loop(0, places // unroll, link, 0)
 
     def term_or_zero(t):
         return jnp.where(t < none, terms[jnp.minimum(t, none - 1)].astype(jnp.float32), 0.0)

time: 80.6 us -> 80.4 us (level)
  no operation moved by 1% of the time
where the time goes in v7:
time: 80.4 us; the launch traced here: 80.3 us
  Pallas kernels  79.6 us (99%)
    pallas_call x1, Pallas kernels, local(): pl.pallas_call(functools.partial(exchange_kernel, chips, span), out_shape...  74.8 us
    pallas_call x1, Pallas kernels, local(): pl.pallas_call(add_kernel, in_specs=[smem, vmem, vmem], out_specs=(anywhe...  4.8 us

profile of v7, /device:TPU:2, one launch (start us, length us, event | category | flops | bytes accessed | tf_op | source)
XLA Modules:
  0.0 80.3 jit_solution(6874547549220034050)
XLA Ops:
  0.6 74.8 %exchange.1 = (bf16[130,128,128]{2,1,0:T(8,128)(2,1)S(1)}, f32[1,128]{1,0:T(1,128)S(1)}, s32[2,65]{1,0:T(2,128)S(4)}) custom-call(f32[1,128]{1,0:T(1,128)} %bitcast.9, s32[64,2,2,64]{3,2,1,0:T(2,128)} %bitcast.8, s32[64,64]{1,0:T(8,128)} %counts_hbm.1, bf16[128,128,128]{2,1,0:T(8,128)(2,1)} %bitcast.6, bf16[64,2,128,128]{3,2,1,0:T(8,128)(2,1)} %bitcast.7), custom_call_target="tpu_custom_call" | custom-call | tf_op jit(solution)/shard_map/exchange/pallas_call | solution.py:459
  75.5 4.8 %add_terms.1 = (f32[128,128,128]{2,1,0:T(8,128)}, f32[1,128]{1,0:T(1,128)}) custom-call(s32[2,65]{1,0:T(2,128)S(4)} %get-tuple-element.7.ids, bf16[130,128,128]{2,1,0:T(8,128)(2,1)S(1)} %get-tuple-element.8.terms, f32[1,128]{1,0:T(1,128)S(1)} %get-tuple-element.9.gain_ref), custom_call_target="tpu_custom_call" | custom-call | tf_op jit(solution)/shard_map/add_terms/pallas_call | solution.py:501
